TPU v7x, 512 devices: a whole 4x8x8 slice. The times are simulated.
512 devices in a mesh: dp: 16 (over z_hi, x, core), ctx: 32 (over y, z_lo).
Axes of the slice: x: 4, y: 8, z: 8 (z_hi: 2, z_lo: 4; z = z_hi * 4 + z_lo), core: 2. Of those that a mesh axis runs over, the one named last changes fastest.
Arguments:
- inputs: bfloat16 [16, 4096, 8192], P('dp', 'ctx'), may hold values from -6 to 6
- queries: bfloat16 [16, 4096, 4096], P('dp', 'ctx'), may hold values from -48 to 48
- upstream: bfloat16 [16, 4096, 4096], P('dp', 'ctx'), may hold values from -6 to 6
- lengths: int32 [16, 32], P('dp'), may hold values from 1 to 384, 4096 in all within a row
- factor_k: bfloat16 [2048, 4, 128], P('ctx'), may hold values from -0.0625 to 0.0625
- factor_v: bfloat16 [2048, 4, 128], P('ctx'), may hold values from -0.0625 to 0.0625
- mixing_k: float32 [4, 4, 4], replicated, may hold values from -3 to 3
- mixing_v: float32 [4, 4, 4], replicated, may hold values from -3 to 3
Outputs:
- grad_factor_k: float32 [2048, 4, 128], P('ctx')
- grad_factor_v: float32 [2048, 4, 128], P('ctx')
- grad_mixing_k: float32 [4, 4, 4], replicated
- grad_mixing_v: float32 [4, 4, 4], replicated
Inputs may be any that keep to these rules, and one draw needn't show every extreme that they name: Each row holds 32 document lengths that sum to 4096; the longest is exactly 384.
All inputs are finite; a program needn't handle non-finite values.
Results may differ from a plain program's by a relative error of at most 0.03.
The roundings to bfloat16 on the way count: a program that leaves them out, or rounds other values in their place, can miss the bound.
Values may be sent and summed in bfloat16 or wider, within the bound.
No kernel may reach another device: no remote copies, remote signals or barrier semaphores. Data moves between devices by JAX's collectives and lax.ppermute only.
A program may use at most 64 MiB of HBM per device.

v0:
```python
import math

import jax
import jax.numpy as jnp
from jax import lax
from jax.sharding import PartitionSpec as P

KVH = 4
HD = 128
REACH = 3
GROUP = 8


def from_behind(block, axis, distance):
    devices = range(lax.axis_size(axis))
    route = [(i - distance, i) for i in devices if i - distance in devices]
    return lax.ppermute(block, axis, route)


def group_grads(qg, dog, kg, vg, mask, scale):
    scores = jnp.einsum("trd,sd->rts", qg, kg, preferred_element_type=jnp.float32) * scale
    scores = jnp.where(mask[None], scores, -1e30)
    top = jnp.max(scores, axis=-1, keepdims=True)
    weights = jnp.exp(scores - top)
    probs = weights / jnp.sum(weights, axis=-1, keepdims=True)
    probs_b = probs.astype(jnp.bfloat16)
    grad_v = jnp.einsum("rts,trd->sd", probs_b, dog, preferred_element_type=jnp.float32)
    dprobs = jnp.einsum("trd,sd->rts", dog, vg, preferred_element_type=jnp.float32)
    delta = jnp.sum(probs * dprobs, axis=-1, keepdims=True)
    dscores = (probs * (dprobs - delta)).astype(jnp.bfloat16)
    grad_k = jnp.einsum("rts,trd->sd", dscores, qg, preferred_element_type=jnp.float32) * scale
    return (grad_k, grad_v)


def fetch_from(keys, values, offset):
    return from_behind((keys, values), "ctx", offset)


def return_from(block_k, block_v, offset):
    return from_behind((block_k, block_v), "ctx", -offset)


def shards(inputs, queries, upstream, lengths, factor_k, factor_v, mixing_k, mixing_v):
    hi = lax.Precision.HIGHEST
    tok = inputs.shape[1]
    width = inputs.shape[2]
    nphm = mixing_k.shape[0]
    cols = factor_k.shape[2]
    e_width = nphm * cols
    dq_rows = width // nphm
    x4 = inputs[0].reshape(tok, nphm, dq_rows)
    span = x4
    part_k = jnp.einsum(
        "tap,piq->itaq",
        span,
        lax.all_gather(factor_k, "ctx", axis=0, tiled=True),
        preferred_element_type=jnp.float32,
    )
    part_v = jnp.einsum(
        "tap,piq->itaq",
        span,
        lax.all_gather(factor_v, "ctx", axis=0, tiled=True),
        preferred_element_type=jnp.float32,
    )
    keys = (
        jnp.einsum("iab,itaq->tbq", mixing_k, part_k, precision=hi)
        .reshape(tok, e_width)
        .astype(jnp.bfloat16)
    )
    values = (
        jnp.einsum("iab,itaq->tbq", mixing_v, part_v, precision=hi)
        .reshape(tok, e_width)
        .astype(jnp.bfloat16)
    )
    fetched = [fetch_from(keys, values, offset) for offset in range(REACH, 0, -1)]
    key_win = jnp.concatenate([item[0] for item in fetched] + [keys], axis=0)
    value_win = jnp.concatenate([item[1] for item in fetched] + [values], axis=0)
    win = key_win.shape[0]
    base = lax.axis_index("ctx") * tok
    ends = jnp.cumsum(lengths[0])
    qpos = base + jnp.arange(tok, dtype=jnp.int32)
    kpos = base - REACH * tok + jnp.arange(win, dtype=jnp.int32)
    qdoc = jnp.sum((ends[None, :] <= qpos[:, None]).astype(jnp.int32), axis=1)
    kdoc = jnp.sum((ends[None, :] <= kpos[:, None]).astype(jnp.int32), axis=1)
    mask = (
        (kpos[None, :] <= qpos[:, None]) & (kpos[None, :] >= 0) & (kdoc[None, :] == qdoc[:, None])
    )
    scale = 1.0 / math.sqrt(HD)
    qg = queries[0].reshape(tok, KVH, GROUP, HD).transpose(1, 0, 2, 3)
    dg = upstream[0].reshape(tok, KVH, GROUP, HD).transpose(1, 0, 2, 3)
    kg = key_win.reshape(win, KVH, HD).transpose(1, 0, 2)
    vg = value_win.reshape(win, KVH, HD).transpose(1, 0, 2)
    grad_k, grad_v = lax.map(
        lambda item: group_grads(item[0], item[1], item[2], item[3], mask, scale), (qg, dg, kg, vg)
    )
    grad_k = grad_k.transpose(1, 0, 2).reshape(REACH + 1, tok, e_width)
    grad_v = grad_v.transpose(1, 0, 2).reshape(REACH + 1, tok, e_width)
    total_k = grad_k[REACH]
    total_v = grad_v[REACH]
    for offset in range(1, REACH + 1):
        recv_k, recv_v = return_from(grad_k[REACH - offset], grad_v[REACH - offset], offset)
        total_k = total_k + recv_k
        total_v = total_v + recv_v
    grad_keys_b = total_k.astype(jnp.bfloat16).astype(jnp.float32).reshape(tok, nphm, cols)
    grad_values_b = total_v.astype(jnp.bfloat16).astype(jnp.float32).reshape(tok, nphm, cols)
    mixed_k = jnp.einsum("iab,tbq->itaq", mixing_k, grad_keys_b, precision=hi).astype(jnp.bfloat16)
    mixed_v = jnp.einsum("iab,tbq->itaq", mixing_v, grad_values_b, precision=hi).astype(
        jnp.bfloat16
    )
    span = x4
    local_k, local_v = jax.tree.map(
        lambda part: lax.psum_scatter(
            part.astype(jnp.bfloat16), "ctx", scatter_dimension=0, tiled=True
        ).astype(jnp.float32),
        (
            jnp.einsum("tap,itaq->piq", span, mixed_k, preferred_element_type=jnp.float32),
            jnp.einsum("tap,itaq->piq", span, mixed_v, preferred_element_type=jnp.float32),
        ),
    )
    grad_fk, grad_fv = lax.psum((local_k, local_v), "dp")
    grad_mk = jnp.einsum("itaq,tbq->iab", part_k, grad_keys_b, precision=hi)
    grad_mv = jnp.einsum("itaq,tbq->iab", part_v, grad_values_b, precision=hi)
    grad_mk, grad_mv = lax.psum((grad_mk, grad_mv), ("dp", "ctx"))
    return (grad_fk, grad_fv, grad_mk, grad_mv)


def solution(mesh):
    in_specs = (
        P("dp", "ctx", None),
        P("dp", "ctx", None),
        P("dp", "ctx", None),
        P("dp", None),
        P("ctx", None, None),
        P("ctx", None, None),
        P(),
        P(),
    )
    out_specs = (P("ctx", None, None), P("ctx", None, None), P(), P())
    return jax.shard_map(shards, mesh=mesh, in_specs=in_specs, out_specs=out_specs, check_vma=False)
```

profile of v0, /device:TPU:1, one launch (start us, length us, event | category | flops | bytes accessed | tf_op | source)
XLA Modules:
  0.0 978.6 jit_solution(9449122848541686878)
XLA Ops:
  7.2 1.5 copy.106
  8.8 1.5 copy.97
  10.4 3.3 reshape_squeeze.9
  15.2 135.7 %all-gather.5.cloned.1.call-done = bf16[2048,4,128]{2,0,1:T(8,128)(2,1)} async-done(((bf16[64,4,128]{2,0,1:T(8,128)(2,1)}), bf16[2048,4,128]{2,0,1:T(8,128)(2,1)}) %all-gather.5.cloned.1.call-update) | async-done | bytes 2097168 | tf_op jit(solution)/shard_map/all_gather | solution.py:62
  150.8 5.7 fusion.81
  156.6 1.8 copy.108
  158.4 1.2 fusion.94
  159.7 1.9 collective-permute-start.3
  161.7 1.9 collective-permute-start.4
  163.6 3.5 collective-permute-start.5
  167.1 141.3 %all-gather.3.cloned.1.call-done = bf16[2048,4,128]{2,0,1:T(8,128)(2,1)} async-done(((bf16[64,4,128]{2,0,1:T(8,128)(2,1)}), bf16[2048,4,128]{2,0,1:T(8,128)(2,1)}) %all-gather.3.cloned.1.call-update) | async-done | bytes 2097168 | tf_op jit(solution)/shard_map/all_gather | solution.py:56
  308.4 5.6 fusion.76
  314.0 1.8 copy.99
  315.9 1.2 fusion.95
  317.2 2.1 collective-permute-start
  319.3 1.9 collective-permute-start.1
  321.3 4.0 collective-permute-start.2
  325.3 2.3 copy.105
  327.6 1.3 copy.114
  328.9 1.1 pad_maximum_fusion.1
  330.0 1.1 pad_maximum_fusion
  331.2 55.1 %while.13 = (s32[]{:T(128)}, f32[4,512,128]{1,2,0:T(8,128)}, f32[4,512,128]{1,2,0:T(8,128)}, bf16[4,512,128]{1,2,0:T(8,128)(2,1)S(1)}, bf16[4,128,8,128]{1,3,2,0...) while((s32[]{:T(128)}, f32[4,512,128]{1,2,0:T(8,128)}, ...), condition=%wide.region_7.8_spmd.clone, body=%wide.region_3.7_spmd.clone.sunk | while | flops 815598080 | bytes 16551605 | solution.py:93
  331.5 3.1 fusion.149
  334.6 3.5 fusion.150
  338.0 3.0 fusion.151
  341.9 3.0 fusion.152
  345.2 3.1 fusion.149
  348.3 3.5 fusion.150
  351.8 3.0 fusion.151
  355.6 3.1 fusion.152
  359.0 3.1 fusion.149
  362.1 3.5 fusion.150
  365.5 3.0 fusion.151
  369.4 3.1 fusion.152
  372.7 3.1 fusion.149
  375.8 3.5 fusion.150
  379.3 3.0 fusion.151
  383.2 3.1 fusion.152
  386.2 1.4 fusion.119
  387.6 1.3 collective-permute-start.10
  388.9 1.3 collective-permute-start.11
  390.2 1.3 collective-permute-start.9
  391.5 0.9 fusion.120
  392.5 1.3 collective-permute-start.6
  393.8 1.3 collective-permute-start.7
  395.1 5.6 collective-permute-done.10
  400.7 1.3 collective-permute-start.8
  402.0 0.9 collective-permute-done.9
  403.1 1.0 fusion.91
  404.0 4.4 fusion.67
  408.4 4.3 copy.129
  412.7 2.0 collective-permute-done.7
  414.9 1.0 fusion.90
  415.8 4.4 fusion.66
  420.2 4.3 copy.124
  424.5 1.4 dynamic-slice
  426.6 335.1 %all-reduce.10.cloned.1.call-done = (bf16[2048,4,128]{2,1,0:T(4,128)(2,1)}, bf16[2048,4,128]{2,1,0:T(4,128)(2,1)}) async-done(((bf16[2048,4,128]{2,1,0:T(4,128)(2,1)}, bf16[2048,4,128]{2,1,0:T(4,128)(2,1)}), (bf16[2048,4,128]{2,1,0:T(4,128)(2,1)}, bf16[2048,4,128]{2,1,0:T(4,128)(2,1)})) %all-reduce.10.cloned.1.call-update) | async-done | bytes 4194320
  761.7 1.6 dynamic-slice_convert_fusion
  763.3 2.3 convolution_bitcast_fusion.4
  765.6 2.3 convolution_bitcast_fusion.5
  768.0 119.0 %all-reduce.2 = (f32[4,4,4]{2,1,0:T(4,128)}, f32[4,4,4]{2,1,0:T(4,128)}) all-reduce(f32[4,4,4]{2,1,0:T(4,128)S(1)} %convolution_bitcast_fusion.5, f32[4,4,4]{2,1,0:T(4,128)S(1)} %convolution_bitcast_fusion.4), channel_id=1, replica_groups=mesh['dp'=16,'ctx'=32] {'dp','ctx'}, use_global_device_ids=true, to_apply=%region_12.13 | all-reduce | flops 128 | bytes 1024 | tf_op jit(solution)/shard_map/psum | solution.py:123
  886.9 82.0 %all-reduce.8.cloned.1.call-done = (f32[64,4,128]{2,1,0:T(4,128)}, f32[64,4,128]{2,1,0:T(4,128)}) async-done(((f32[64,4,128]{2,1,0:T(4,128)}, f32[64,4,128]{2,1,0:T(4,128)}), (f32[64,4,128]{2,1,0:T(4,128)}, f32[64,4,128]{2,1,0:T(4,128)})) %all-reduce.8.cloned.1.call-update) | async-done | bytes 262160 | tf_op jit(solution)/shard_map/psum | solution.py:120
  969.0 1.6 copy.213
  970.5 1.6 copy.214
  (83 shorter events, 7.0 us)
Async XLA Ops:
  7.2 151.2 %copy-start = (f32[4,4,4]{2,1,0:T(4,128)S(1)}, f32[4,4,4]{2,1,0:T(4,128)}, u32[]{:S(2)}) copy-start(f32[4,4,4]{2,1,0:T(4,128)} %param.17) | copy-start | bytes 772
  7.2 143.7 %all-gather.5.cloned.1.call-start = ((), (), s32[]{:S(2)}) async-start(), calls=%async_computation.1 | async-start | bytes 2162688 | tf_op jit(solution)/shard_map/all_gather | solution.py:62
  8.7 299.7 %all-gather.3.cloned.1.call-start = ((), (), s32[]{:S(2)}) async-start(), calls=%async_computation | async-start | bytes 2162688 | tf_op jit(solution)/shard_map/all_gather | solution.py:56
  10.3 751.4 %all-reduce.10.cloned.1.call-start = ((), (), s32[]{:S(2)}) async-start(), calls=%async_computation.3 | async-start | bytes 8388608
  10.3 3.3 copy-start.12
  14.0 0.5 copy-start.9
  159.7 161.5 %collective-permute-start.3 = (bf16[128,512]{0,1:T(8,128)(2,1)S(1)}, bf16[128,512]{0,1:T(8,128)(2,1)}, u32[]{:S(2)}, u32[]{:S(2)}) collective-permute-start(bf16[128,512]{0,1:T(8,128)(2,1)S(1)} %bitcast.288), channel_id=1, source_target_pairs={{0,3},{1,4},{2,5},{3,6},{4,7},{5,8},{6,9},{7,10},{8,11},{9,12},{10... | collective-permute-start | bytes 393224 | tf_op jit(solution)/shard_map/ppermute | solution.py:17
  161.7 167.2 %collective-permute-start.4 = (bf16[128,512]{0,1:T(8,128)(2,1)S(1)}, bf16[128,512]{0,1:T(8,128)(2,1)}, u32[]{:S(2)}, u32[]{:S(2)}) collective-permute-start(bf16[128,512]{0,1:T(8,128)(2,1)S(1)} %bitcast.289), channel_id=1, source_target_pairs={{0,2},{1,3},{2,4},{3,5},{4,6},{5,7},{6,8},{7,9},{8,10},{9,11},{10,... | collective-permute-start | bytes 393224 | tf_op jit(solution)/shard_map/ppermute | solution.py:17
  163.6 165.3 %collective-permute-start.5 = (bf16[128,512]{0,1:T(8,128)(2,1)S(1)}, bf16[128,512]{0,1:T(8,128)(2,1)}, u32[]{:S(2)}, u32[]{:S(2)}) collective-permute-start(bf16[128,512]{0,1:T(8,128)(2,1)S(1)} %bitcast.290), channel_id=1, source_target_pairs={{0,1},{1,2},{2,3},{3,4},{4,5},{5,6},{6,7},{7,8},{8,9},{9,10},{10,1... | collective-permute-start | bytes 393224 | tf_op jit(solution)/shard_map/ppermute | solution.py:17
  314.0 1.9 copy-start.7
  317.1 10.5 %copy-start.1 = (bf16[1,128,4096]{2,1,0:T(8,128)(2,1)S(1)}, bf16[1,128,4096]{2,1,0:T(8,128)(2,1)}, u32[]{:S(2)}) copy-start(bf16[1,128,4096]{2,1,0:T(8,128)(2,1)} %param.12) | copy-start | bytes 3145732
  317.2 12.8 %collective-permute-start = (bf16[128,512]{0,1:T(8,128)(2,1)S(1)}, bf16[128,512]{0,1:T(8,128)(2,1)}, u32[]{:S(2)}, u32[]{:S(2)}) collective-permute-start(bf16[128,512]{0,1:T(8,128)(2,1)S(1)} %bitcast.292), channel_id=1, source_target_pairs={{0,3},{1,4},{2,5},{3,6},{4,7},{5,8},{6,9},{7,10},{8,11},{9,12},{10... | collective-permute-start | bytes 393224 | tf_op jit(solution)/shard_map/ppermute | solution.py:17
  319.3 10.7 %collective-permute-start.1 = (bf16[128,512]{0,1:T(8,128)(2,1)S(1)}, bf16[128,512]{0,1:T(8,128)(2,1)}, u32[]{:S(2)}, u32[]{:S(2)}) collective-permute-start(bf16[128,512]{0,1:T(8,128)(2,1)S(1)} %bitcast.293), channel_id=1, source_target_pairs={{0,2},{1,3},{2,4},{3,5},{4,6},{5,7},{6,8},{7,9},{8,10},{9,11},{10,... | collective-permute-start | bytes 393224 | tf_op jit(solution)/shard_map/ppermute | solution.py:17
  321.3 8.8 collective-permute-start.2
  327.6 3.6 copy-start.10
  327.6 3.6 copy-start.11
  331.2 6.8 copy-start.5
  341.9 3.0 copy-start.6
  344.9 6.8 copy-start.5
  355.6 3.1 copy-start.6
  358.7 6.8 copy-start.5
  369.4 3.1 copy-start.6
  372.5 6.8 copy-start.5
  383.2 3.1 copy-start.6
  386.2 5.3 copy-start.4
  387.6 13.0 %collective-permute-start.10 = (f32[128,512]{0,1:T(8,128)S(1)}, f32[128,512]{0,1:T(8,128)S(1)}, u32[]{:S(2)}, u32[]{:S(2)}) collective-permute-start(f32[128,512]{0,1:T(8,128)S(1)} %bitcast.298), channel_id=1, source_target_pairs={{2,0},{3,1},{4,2},{5,3},{6,4},{7,5},{8,6},{9,7},{10,8},{11,9},{12,... | collective-permute-start | bytes 786440 | tf_op jit(solution)/shard_map/ppermute | solution.py:17
  388.9 13.0 %collective-permute-start.11 = (f32[128,512]{0,1:T(8,128)S(1)}, f32[128,512]{0,1:T(8,128)S(1)}, u32[]{:S(2)}, u32[]{:S(2)}) collective-permute-start(f32[128,512]{0,1:T(8,128)S(1)} %bitcast.297), channel_id=1, source_target_pairs={{3,0},{4,1},{5,2},{6,3},{7,4},{8,5},{9,6},{10,7},{11,8},{12,9},{13... | collective-permute-start | bytes 786440 | tf_op jit(solution)/shard_map/ppermute | solution.py:17
  390.2 12.6 %collective-permute-start.9 = (f32[128,512]{0,1:T(8,128)S(1)}, f32[128,512]{0,1:T(8,128)S(1)}, u32[]{:S(2)}, u32[]{:S(2)}) collective-permute-start(f32[128,512]{0,1:T(8,128)S(1)} %bitcast.296), channel_id=1, source_target_pairs={{1,0},{2,1},{3,2},{4,3},{5,4},{6,5},{7,6},{8,7},{9,8},{10,9},{11,1... | collective-permute-start | bytes 786440 | tf_op jit(solution)/shard_map/ppermute | solution.py:17
  392.5 20.2 %collective-permute-start.6 = (f32[128,512]{0,1:T(8,128)}, f32[128,512]{0,1:T(8,128)S(1)}, u32[]{:S(2)}, u32[]{:S(2)}) collective-permute-start(f32[128,512]{0,1:T(8,128)} %bitcast.27), channel_id=1, source_target_pairs={{1,0},{2,1},{3,2},{4,3},{5,4},{6,5},{7,6},{8,7},{9,8},{10,9},{11,1... | collective-permute-start | bytes 786440 | tf_op jit(solution)/shard_map/ppermute | solution.py:17
  393.8 20.9 %collective-permute-start.7 = (f32[128,512]{0,1:T(8,128)}, f32[128,512]{0,1:T(8,128)S(1)}, u32[]{:S(2)}, u32[]{:S(2)}) collective-permute-start(f32[128,512]{0,1:T(8,128)} %bitcast.28), channel_id=1, source_target_pairs={{2,0},{3,1},{4,2},{5,3},{6,4},{7,5},{8,6},{9,7},{10,8},{11,9},{12,... | collective-permute-start | bytes 786440 | tf_op jit(solution)/shard_map/ppermute | solution.py:17
  400.7 14.0 %collective-permute-start.8 = (f32[128,512]{0,1:T(8,128)}, f32[128,512]{0,1:T(8,128)S(1)}, u32[]{:S(2)}, u32[]{:S(2)}) collective-permute-start(f32[128,512]{0,1:T(8,128)} %bitcast.29), channel_id=1, source_target_pairs={{3,0},{4,1},{5,2},{6,3},{7,4},{8,5},{9,6},{10,7},{11,8},{12,9},{13... | collective-permute-start | bytes 786440 | tf_op jit(solution)/shard_map/ppermute | solution.py:17
  408.4 6.5 copy-start.8
  424.5 338.9 %copy-start.2 = (f32[4,128,4,128]{1,3,2,0:T(8,128)S(1)}, f32[4,128,4,128]{1,3,2,0:T(8,128)}, u32[]{:S(2)}) copy-start(f32[4,128,4,128]{1,3,2,0:T(8,128)} %fusion.81) | copy-start | bytes 3145732
  424.5 341.2 %copy-start.3 = (f32[4,128,4,128]{1,3,2,0:T(8,128)S(1)}, f32[4,128,4,128]{1,3,2,0:T(8,128)}, u32[]{:S(2)}) copy-start(f32[4,128,4,128]{1,3,2,0:T(8,128)} %fusion.76) | copy-start | bytes 3145732
  424.5 544.5 %all-reduce.8.cloned.1.call-start = ((), (), s32[]{:S(2)}) async-start(), calls=%async_computation.2 | async-start | bytes 524288 | tf_op jit(solution)/shard_map/psum | solution.py:120
Sparse Core Ops, SparseCore 0:
  10.7 140.1 all-gather.4
  153.5 154.8 all-gather.2
  424.6 337.0 all-reduce.9
  765.1 203.8 all-reduce.7
where the time goes:
time: 980 us; the launch traced here: 979 us
  waiting for transfers between devices  703 us (72%)
  blocking collectives  119 us (12%)
  matrix products  79.3 us (8%)
  local copies, waits for them, and re-layouts  33.6 us (3%)
  starting transfers between devices  23.3 us (2%)
  between operations  14.7 us (2%)
    unnamed x5, waiting for transfers between devices  335 us
    all_gather x1, waiting for transfers between devices, shards(): lax.all_gather(factor_k, 'ctx', axis=0, tiled=True)  141 us
    all_gather x1, waiting for transfers between devices, shards(): lax.all_gather(factor_v, 'ctx', axis=0, tiled=True)  136 us
    psum x1, blocking collectives, shards(): grad_mk, grad_mv = lax.psum((grad_mk, grad_mv), ('dp', 'ctx'))  119 us
    psum x1, waiting for transfers between devices, shards(): grad_fk, grad_fv = lax.psum((local_k, local_v), 'dp')  82 us
    ppermute x12, starting transfers between devices, from_behind(): return lax.ppermute(block, axis, route)  23.1 us
  transfers between devices with their start and end apart: 16, of which 7 were waited for; matrix products, arithmetic and copies ran while one was open for 5% of the time, Pallas kernels for 0%

commit v1 on v0

v1 whole, which is shorter than its diff:
```python
import functools
import math

import jax
import jax.numpy as jnp
from jax import lax
from jax.experimental import pallas as pl
from jax.experimental.pallas import tpu as pltpu
from jax.sharding import Mesh, PartitionSpec as P

KVH = 4
HD = 128
REACH = 3
GROUP = 8
NPHM = 4
PAD = 16
CTX = ("y", "zl")
DP = ("zh", "x", "c")
SCALE = 1.0 / math.sqrt(HD)
LOG2E = 1.4426950408889634
SMEM = pl.BlockSpec(memory_space=pltpu.SMEM)
F32 = jnp.float32
BF16 = jnp.bfloat16


def dot(a, b, ca, cb):
    return lax.dot_general(a, b, (((ca,), (cb,)), ((), ())), preferred_element_type=F32)


def params(mib):
    return pltpu.CompilerParams(vmem_limit_bytes=mib << 20)


def project_kernel(mix, xm, xo, w, part, out, wide, acc):
    a = pl.program_id(0)

    @pl.when(a == 0)
    def _():
        for i in range(NPHM):
            wide[:, i * HD : (i + 1) * HD] = w[i]
        acc[...] = jnp.zeros_like(acc)

    x = jnp.concatenate([xm[0], xo[0]], axis=0)
    one = dot(x, wide[...], 1, 0)
    part[0] = one
    for b in range(NPHM):
        at = slice(b * HD, (b + 1) * HD)
        total = acc[:, at]
        for i in range(NPHM):
            total = total + mix[i * 16 + a * 4 + b] * one[:, i * HD : (i + 1) * HD]
        acc[:, at] = total

    @pl.when(a == NPHM - 1)
    def _():
        tok = xm.shape[1]
        out[0] = acc[:tok].astype(BF16)
        out[1] = acc[tok:].astype(BF16)


def project(mix, xm, xo, w):
    tok, width = xm.shape[1:]
    dq, cols = width // NPHM, NPHM * HD
    return pl.pallas_call(
        project_kernel,
        grid=(NPHM,),
        in_specs=[
            SMEM,
            pl.BlockSpec((1, tok, dq), lambda a: (0, 0, a)),
            pl.BlockSpec((1, tok, dq), lambda a: (0, 0, a)),
            pl.BlockSpec((NPHM, dq, HD), lambda a: (0, 0, 0)),
        ],
        out_specs=[
            pl.BlockSpec((1, 2 * tok, cols), lambda a: (a, 0, 0)),
            pl.BlockSpec((2, tok, cols), lambda a: (0, 0, 0)),
        ],
        out_shape=[
            jax.ShapeDtypeStruct((NPHM, 2 * tok, cols), F32),
            jax.ShapeDtypeStruct((2, tok, cols), BF16),
        ],
        scratch_shapes=[pltpu.VMEM((dq, cols), BF16), pltpu.VMEM((2 * tok, cols), F32)],
        compiler_params=params(40),
    )(mix, xm, xo, w)


def attend_kernel(base, lens, q, do, w3, w2, w1, w0, s3, s2, s1, own, bias, probs, dscores):
    tok = q.shape[1]
    win = (REACH + 1) * tok

    @pl.when(pl.program_id(0) == 0)
    def _():
        start = base[0]
        qpos = start + lax.broadcasted_iota(jnp.int32, (8, tok), 1)

        def step(n, carry):
            end, first = carry
            end = end + lens[n]
            return end, jnp.where(end <= qpos, end, first)

        _, first = lax.fori_loop(
            0, lens.shape[0], step, (jnp.int32(0), jnp.zeros((8, tok), jnp.int32))
        )
        kpos = start - REACH * tok + lax.broadcasted_iota(jnp.int32, (win, tok), 0)
        ok = (kpos >= first[0:1]) & (kpos <= qpos[0:1])
        bias[...] = jnp.where(ok, 0.0, -1e30).astype(F32)

    k = jnp.concatenate([w[0] for w in (w3, w2, w1, w0)], axis=0)
    v = jnp.concatenate([w[1] for w in (w3, w2, w1, w0)], axis=0)
    for r in range(GROUP):
        at = slice(r * HD, (r + 1) * HD)
        rows = slice(r * tok, (r + 1) * tok)
        s = dot(k, q[0, :, at], 1, 1) * (SCALE * LOG2E) + bias[...]
        dp = dot(v, do[0, :, at], 1, 1)
        e = jnp.exp2(s - jnp.max(s, axis=0, keepdims=True))
        p = e * (1.0 / jnp.sum(e, axis=0, keepdims=True))
        delta = jnp.sum(p * dp, axis=0, keepdims=True)
        probs[:, rows] = p.astype(BF16)
        dscores[:, rows] = (p * (dp - delta)).astype(BF16)
    qs = jnp.concatenate([q[0, :, r * HD : (r + 1) * HD] for r in range(GROUP)], axis=0)
    dos = jnp.concatenate([do[0, :, r * HD : (r + 1) * HD] for r in range(GROUP)], axis=0)
    gk = dot(dscores[...], qs, 1, 0) * SCALE
    gv = dot(probs[...], dos, 1, 0)
    for n, out in enumerate((s3, s2, s1)):
        out[0] = gk[n * tok : (n + 1) * tok].astype(BF16)
        out[1] = gv[n * tok : (n + 1) * tok].astype(BF16)
    own[0] = gk[REACH * tok :]
    own[1] = gv[REACH * tok :]


def attend(base, lens, q, do, wins):
    tok = q.shape[1]
    win = (REACH + 1) * tok
    wide = GROUP * HD
    head = pl.BlockSpec((1, tok, wide), lambda g: (0, 0, g))
    run = pl.BlockSpec((2, tok, HD), lambda g: (0, 0, g))
    shape = (2, tok, KVH * HD)
    return pl.pallas_call(
        attend_kernel,
        grid=(KVH,),
        in_specs=[SMEM, SMEM, head, head] + [run] * 4,
        out_specs=[run] * 4,
        out_shape=[jax.ShapeDtypeStruct(shape, BF16)] * 3 + [jax.ShapeDtypeStruct(shape, F32)],
        scratch_shapes=[
            pltpu.VMEM((win, tok), F32),
            pltpu.VMEM((win, GROUP * tok), BF16),
            pltpu.VMEM((win, GROUP * tok), BF16),
        ],
        compiler_params=params(40),
    )(base, lens, q, do, *wins)


def factor_kernel(mix, *refs):
    xs, (gm, go, part, out, row, mixed, grads) = refs[:8], refs[8:]
    j = pl.program_id(0)
    tok = gm.shape[0]

    @pl.when(j == 0)
    def _():
        grads[:tok] = gm[...].astype(F32)
        grads[tok:] = go[...].astype(F32)
        for a in range(NPHM):
            for i in range(NPHM):
                total = mix[i * 16 + a * 4] * grads[:, :HD]
                for b in range(1, NPHM):
                    total = total + mix[i * 16 + a * 4 + b] * grads[:, b * HD : (b + 1) * HD]
                mixed[a, :, i * HD : (i + 1) * HD] = total.astype(BF16)
        sums = []
        for i in range(NPHM):
            for a in range(NPHM):
                for b in range(NPHM):
                    both = part[a, :, i * HD : (i + 1) * HD] * grads[:, b * HD : (b + 1) * HD]
                    sums.append(jnp.sum(both, axis=0, keepdims=True))
        sums = jnp.sum(jnp.concatenate(sums, axis=0), axis=1, keepdims=True)
        many = NPHM**3
        spot = lax.broadcasted_iota(jnp.int32, (many, 2 * many), 0)
        lane = lax.broadcasted_iota(jnp.int32, (many, 2 * many), 1)
        line = jnp.sum(jnp.where(spot == lane, sums, 0.0), axis=0, keepdims=True)
        row[...] = jnp.broadcast_to(line, row.shape)

    total = None
    for a in range(NPHM):
        x = jnp.concatenate([xs[a][0], xs[4 + a][0]], axis=0)
        one = dot(mixed[a], x, 0, 0)
        total = one if total is None else total + one
    for i in range(NPHM):
        out[i] = total[i * HD : (i + 1) * HD].astype(BF16)


def factor_grads(mix, xm, xo, gm, go, part):
    tok, width = xm.shape[1:]
    dq, cols = width // NPHM, NPHM * HD
    steps = 4
    wide = dq // steps
    xspecs = [
        pl.BlockSpec((1, tok, wide), functools.partial(lambda a, j: (0, 0, a * steps + j), a))
        for a in range(NPHM)
    ]
    whole = pl.BlockSpec((tok, cols), lambda j: (0, 0))
    return pl.pallas_call(
        factor_kernel,
        grid=(steps,),
        in_specs=[SMEM]
        + xspecs
        + xspecs
        + [whole, whole, pl.BlockSpec((NPHM, 2 * tok, cols), lambda j: (0, 0, 0))],
        out_specs=[
            pl.BlockSpec((NPHM, HD, wide), lambda j: (0, 0, j)),
            pl.BlockSpec((8, HD), lambda j: (0, 0)),
        ],
        out_shape=[
            jax.ShapeDtypeStruct((NPHM, HD, dq), BF16),
            jax.ShapeDtypeStruct((8, HD), F32),
        ],
        scratch_shapes=[
            pltpu.VMEM((NPHM, 2 * tok, cols), BF16),
            pltpu.VMEM((2 * tok, cols), F32),
        ],
        compiler_params=params(40),
    )(mix, *([xm] * 4), *([xo] * 4), gm, go, part)


def split_line(value):
    lane = lax.broadcasted_iota(jnp.int32, value.shape, 1)
    high = value.astype(BF16).astype(F32)
    return jnp.where(lane < HD // 2, high, value - high)


def turn_kernel(terms, row, out):
    n, rows = out.shape[0], out.shape[1] - PAD
    total = terms[0].astype(F32)
    for i in range(1, NPHM):
        total = total + terms[i].astype(F32)
    turned = total.T.astype(BF16)
    line = row[0:1]
    line = line + jnp.concatenate([line[:, HD // 2 :], line[:, : HD // 2]], axis=1)
    line = jnp.broadcast_to(split_line(line), (PAD, HD)).astype(BF16)
    for d in range(n):
        out[d, :rows] = turned[d * rows : (d + 1) * rows]
        out[d, rows:] = line


def turn(terms, row, n):
    rows = terms.shape[2] // n
    return pl.pallas_call(
        turn_kernel,
        out_shape=jax.ShapeDtypeStruct((n, rows + PAD, HD), BF16),
        compiler_params=params(40),
    )(terms, row)


def total_kernel(blocks, out):
    rows = out.shape[1] - PAD
    total = blocks[0].astype(F32)
    for d in range(1, blocks.shape[0]):
        total = total + blocks[d].astype(F32)
    line = total[rows : rows + 1]
    line = line + jnp.concatenate([line[:, HD // 2 :], line[:, : HD // 2]], axis=1)
    line = jnp.broadcast_to(split_line(line), (PAD, HD)).astype(BF16)
    body = total[:rows].astype(BF16)
    for d in range(out.shape[0]):
        out[d, :rows] = body
        out[d, rows:] = line


def total(blocks, n):
    return pl.pallas_call(
        total_kernel,
        out_shape=jax.ShapeDtypeStruct((n,) + blocks.shape[1:], BF16),
        compiler_params=params(40),
    )(blocks)


def shards(inputs, queries, upstream, lengths, factor_k, factor_v, mixing_k, mixing_v):
    tok = inputs.shape[1]
    rows = factor_k.shape[0]
    n_ctx = lax.axis_size("y") * lax.axis_size("zl")
    n_dp = lax.axis_size("zh") * lax.axis_size("x") * lax.axis_size("c")
    ctx = lax.axis_index("y") * lax.axis_size("zl") + lax.axis_index("zl")
    x_at = lax.axis_index("x")
    first = lax.axis_index("c") == 0
    swap = [(0, 1), (1, 0)]

    other = lax.ppermute(inputs, "c", swap)
    mix = jnp.where(first, mixing_k, mixing_v).reshape(-1)
    mine = lax.dynamic_index_in_dim(
        jnp.where(first, factor_k, factor_v), x_at, axis=1, keepdims=False
    )
    piece = jnp.broadcast_to(mine[None], (n_ctx, rows, HD))
    piece = lax.all_to_all(piece, CTX, 0, 0, tiled=True).reshape(1, n_ctx * rows, HD)
    weights = lax.all_to_all(
        jnp.broadcast_to(piece, (NPHM, n_ctx * rows, HD)), "x", 0, 0, tiled=True
    )
    part, both = project(mix, inputs, other, weights)

    got = lax.ppermute(both[1], "c", swap)
    pack = jnp.stack([jnp.where(first, both[0], got), jnp.where(first, got, both[0])])
    wins = []
    for d in range(REACH, 0, -1):
        route = [(n - d, n) for n in range(d, n_ctx)]
        wins.append(lax.ppermute(pack, CTX, route))
    base = (ctx * tok).astype(jnp.int32).reshape(1)
    *away, own = attend(base, lengths[0], queries, upstream, wins + [pack])
    for d, block in zip(range(REACH, 0, -1), away):
        route = [(n, n - d) for n in range(d, n_ctx)]
        own = own + lax.ppermute(block, CTX, route).astype(F32)
    grads = own.astype(BF16)
    keep = jnp.where(first, grads[0], grads[1])
    got = lax.ppermute(jnp.where(first, grads[1], grads[0]), "c", swap)

    terms, row = factor_grads(mix, inputs, other, keep, got, part)
    terms = lax.all_to_all(terms, "x", 0, 0, tiled=True)
    blocks = lax.all_to_all(turn(terms, row, n_ctx), CTX, 0, 0, tiled=True)
    blocks = lax.all_to_all(total(blocks, n_dp), DP, 0, 0, tiled=True)
    blocks = blocks.reshape(lax.axis_size("zh"), NPHM, 2, rows + PAD, HD).astype(F32)
    blocks = jnp.sum(blocks, axis=0)
    grad_f = blocks[:, :, :rows].transpose(1, 2, 0, 3)
    lines = jnp.sum(blocks[:, :, rows], axis=0)
    lines = lines[:, : HD // 2] + lines[:, HD // 2 :]
    grad_m = lines.reshape(2, NPHM, NPHM, NPHM)
    return (grad_f[0], grad_f[1], grad_m[0], grad_m[1])


def solution(mesh):
    n_dp, n_ctx = mesh.devices.shape
    zl = 4
    shape = (n_dp // 8, 4, 2, n_ctx // zl, zl)
    wide = Mesh(mesh.devices.reshape(shape), DP + CTX)
    in_specs = (
        P(DP, CTX, None),
        P(DP, CTX, None),
        P(DP, CTX, None),
        P(DP, None),
        P(CTX, None, None),
        P(CTX, None, None),
        P(),
        P(),
    )
    out_specs = (P(CTX, None, None), P(CTX, None, None), P(), P())
    return jax.shard_map(shards, mesh=wide, in_specs=in_specs, out_specs=out_specs, check_vma=False)
```

time: 980 us -> 242 us (0.25)
  waiting for transfers between devices: 703 us -> 75.3 us
  matrix products: 79.3 us -> 0 us
  blocking collectives: 119 us -> 86.9 us
  Pallas kernels: 0 us -> 24.6 us
  local copies, waits for them, and re-layouts: 33.6 us -> 9.11 us
  starting transfers between devices: 23.3 us -> 43.2 us
  between operations: 14.7 us -> 0.85 us
    unnamed x5 -> x0, waiting for transfers between devices: 335 us -> none
    all_gather x2 -> x0, waiting for transfers between devices: 277 us -> none  [the longest x1 141 us: shards(): lax.all_gather(factor_k, 'ctx', axis=0, tiled=True)]
    psum x1 -> x0, blocking collectives: 119 us -> none  [shards(): grad_mk, grad_mv = lax.psum((grad_mk, grad_mv), ('dp', 'ctx'))]
    all_to_all x0 -> x3, blocking collectives: none -> 86.9 us  [the longest x1 35 us: shards(): blocks = lax.all_to_all(turn(terms, row, n_ctx), CTX, 0, 0, tiled=True)]
    psum x1 -> x0, waiting for transfers between devices: 82 us -> none  [shards(): grad_fk, grad_fv = lax.psum((local_k, local_v), 'dp')]
    dot_general x22 -> x0, matrix products: 67 us -> none  [the longest x4 13.8 us: group_grads(): jnp.einsum('trd,sd->rts', dog, vg, preferred_element_type=jnp.float32)]
    all_to_all x0 -> x2, waiting for transfers between devices: none -> 37.3 us  [the longest x1 23.6 us: shards(): lax.all_to_all(jnp.broadcast_to(piece, (NPHM, n_ctx * rows, HD)), 'x', 0,...]
    ppermute x12 -> x9, waiting for transfers between devices: 8.48 us -> 38 us  [the longest x3 26.8 us: shards(): own = own + lax.ppermute(block, CTX, route).astype(F32)]
  transfers between devices with their start and end apart: 16 -> 11, of which waited for: 7 -> 8; matrix products, arithmetic and copies ran while one was open for 5% -> 1% of each run, Pallas kernels for 0% -> 0%
where the time goes in v1:
time: 242 us; the launch traced here: 240 us
  blocking collectives  86.9 us (36%)
  waiting for transfers between devices  75.3 us (31%)
  starting transfers between devices  43.2 us (18%)
  Pallas kernels  24.6 us (10%)
  local copies, waits for them, and re-layouts  9.11 us (4%)
    all_to_all x1, blocking collectives, shards(): blocks = lax.all_to_all(turn(terms, row, n_ctx), CTX, 0, 0, tiled=True)  35 us
    all_to_all x1, blocking collectives, shards(): terms = lax.all_to_all(terms, 'x', 0, 0, tiled=True)  28.6 us
    ppermute x3, waiting for transfers between devices, shards(): own = own + lax.ppermute(block, CTX, route).astype(F32)  26.8 us
    all_to_all x1, waiting for transfers between devices, shards(): lax.all_to_all(jnp.broadcast_to(piece, (NPHM, n_ctx * rows, HD)), 'x', 0,...  23.6 us
    all_to_all x1, blocking collectives, shards(): blocks = lax.all_to_all(total(blocks, n_dp), DP, 0, 0, tiled=True)  23.3 us
    all_to_all x1, waiting for transfers between devices, shards(): lax.all_to_all(piece, CTX, 0, 0, tiled=True).reshape(1, n_ctx * rows, HD)  13.7 us
    all_to_all x1, starting transfers between devices, shards(): lax.all_to_all(piece, CTX, 0, 0, tiled=True).reshape(1, n_ctx * rows, HD)  13.5 us
    pallas_call x1, Pallas kernels, attend(): pl.pallas_call(attend_kernel, grid=(KVH,), in_specs=[SMEM, SMEM, head, he...  11.9 us
  transfers between devices with their start and end apart: 11, of which 8 were waited for; matrix products, arithmetic and copies ran while one was open for 1% of the time, Pallas kernels for 0%

profile of v1, /device:TPU:1, one launch (start us, length us, event | category | flops | bytes accessed | tf_op | source)
XLA Modules:
  0.0 240.3 jit_solution(9592538377619529558)
XLA Ops:
  0.6 0.9 constant_dynamic-slice_fusion
  1.6 0.9 broadcast_in_dim.16
  2.5 13.5 %all-to-all-start = ((bf16[32,64,128]{2,1,0:T(8,128)(2,1)}), bf16[32,64,128]{2,1,0:T(8,128)(2,1)S(1)}, u32[]{:S(2)}, u32[]{:S(2)}) async-start(bf16[32,64,128]{2,1,0:T(8,128)(2,1)} %broadcast_in_dim.16), calls=%async_computation | async-start | bytes 1048576 | tf_op jit(solution)/shard_map/all_to_all | solution.py:288
  16.0 2.9 %collective-permute-start = (bf16[1,128,8192]{2,1,0:T(8,128)(2,1)}, bf16[1,128,8192]{2,1,0:T(8,128)(2,1)}, u32[]{:S(2)}, u32[]{:S(2)}) collective-permute-start(bf16[1,128,8192]{2,1,0:T(8,128)(2,1)} %refs_3_.1), channel_id=1, source_target_pairs={{0,32},{32,0},{1,33},{33,1},{2,34},{34,2},{3,35},{35,3},{4,36},{36... | collective-permute-start | bytes 6291464 | tf_op jit(solution)/shard_map/ppermute | solution.py:282
  18.9 13.7 %all-to-all-done = bf16[32,64,128]{2,1,0:T(8,128)(2,1)S(1)} async-done(((bf16[32,64,128]{2,1,0:T(8,128)(2,1)}), bf16[32,64,128]{2,1,0:T(8,128)(2,1)S(1)}, u32[]{:S(2)}, u32[]{:S(2)}) %all-to-all-start) | async-done | bytes 524320 | tf_op jit(solution)/shard_map/all_to_all | solution.py:288
  32.6 1.6 broadcast_in_dim.18
  34.2 0.0 copy-start.6
  34.2 0.0 copy-start.7
  34.2 0.0 copy-start
  34.2 4.6 %all-to-all-start.1 = ((bf16[4,2048,128]{2,1,0:T(8,128)(2,1)}), bf16[4,2048,128]{2,1,0:T(8,128)(2,1)}, u32[]{:S(2)}, u32[]{:S(2)}) async-start(bf16[4,2048,128]{2,1,0:T(8,128)(2,1)} %broadcast_in_dim.18), calls=%async_computation.1 | async-start | bytes 4194304 | tf_op jit(solution)/shard_map/all_to_all | solution.py:289
  38.8 0.0 copy-done.6
  38.8 0.0 copy-done.7
  38.9 0.1 reshape.30.mix
  38.9 0.0 copy-start.3
  39.0 0.0 copy-start.5
  39.0 0.0 collective-permute-done.xo.refs_4_.refs_5_.refs_6_.refs_7_
  39.0 23.6 %all-to-all-done.1.w = bf16[4,2048,128]{2,1,0:T(8,128)(2,1)} async-done(((bf16[4,2048,128]{2,1,0:T(8,128)(2,1)}), bf16[4,2048,128]{2,1,0:T(8,128)(2,1)}, u32[]{:S(2)}, u32[]{:S(2)}) %all-to-all-start.1) | async-done | bytes 2097184 | tf_op jit(solution)/shard_map/all_to_all | solution.py:289
  62.6 0.0 copy-done
  62.6 5.9 %shard_map.111 = (f32[4,256,512]{2,1,0:T(8,128)S(1)}, bf16[2,128,512]{2,1,0:T(8,128)(2,1)S(1)}) custom-call(f32[64]{0:T(128)S(1)} %reshape.30.mix, bf16[1,128,8192]{2,1,0:T(8,128)(2,1)S(1)} %copy-done, bf16[1,128,8192]{2,1,0:T(8,128)(2,1)} %collective-permute-done.xo.refs_4_.refs_5_.refs_6_.refs_7_, bf16[4,2048,128]{2,1,0:T(8,128)(2,1)} %all-to-all-done.1.w), custom_call_target="tpu_custom_call" | custom-call | tf_op jit(solution)/shard_map/pallas_call | solution.py:63
  68.4 0.0 copy-start.1
  68.4 1.3 copy-done.1
  69.8 5.5 %collective-permute-start.1 = (bf16[128,512]{1,0:T(8,128)(2,1)S(1)}, bf16[128,512]{1,0:T(8,128)(2,1)S(1)}, u32[]{:S(2)}, u32[]{:S(2)}) collective-permute-start(bf16[128,512]{1,0:T(8,128)(2,1)S(1)} %slice_bitcast_fusion.3), channel_id=1, source_target_pairs={{0,32},{32,0},{1,33},{33,1},{2,34},{34,2},{3,35},{35,3},{4,36},{36... | collective-permute-start | bytes 393224 | tf_op jit(solution)/shard_map/ppermute | solution.py:294
  75.3 1.0 collective-permute-done.1
  76.3 3.4 %collective-permute-start.4 = (bf16[2,128,512]{2,1,0:T(8,128)(2,1)S(1)}, bf16[2,128,512]{2,1,0:T(8,128)(2,1)}, u32[]{:S(2)}, u32[]{:S(2)}) collective-permute-start(bf16[2,128,512]{2,1,0:T(8,128)(2,1)S(1)} %pad_maximum_fusion.w0), channel_id=1, source_target_pairs={{0,1},{1,2},{2,3},{3,4},{4,5},{5,6},{6,7},{7,8},{8,9},{9,10},{10,1... | collective-permute-start | bytes 786440 | tf_op jit(solution)/shard_map/ppermute | solution.py:299
  79.7 3.6 %collective-permute-start.3 = (bf16[2,128,512]{2,1,0:T(8,128)(2,1)S(1)}, bf16[2,128,512]{2,1,0:T(8,128)(2,1)}, u32[]{:S(2)}, u32[]{:S(2)}) collective-permute-start(bf16[2,128,512]{2,1,0:T(8,128)(2,1)S(1)} %pad_maximum_fusion.w0), channel_id=1, source_target_pairs={{0,2},{1,3},{2,4},{3,5},{4,6},{5,7},{6,8},{7,9},{8,10},{9,11},{10,... | collective-permute-start | bytes 786440 | tf_op jit(solution)/shard_map/ppermute | solution.py:299
  83.4 2.9 %collective-permute-start.2 = (bf16[2,128,512]{2,1,0:T(8,128)(2,1)S(1)}, bf16[2,128,512]{2,1,0:T(8,128)(2,1)}, u32[]{:S(2)}, u32[]{:S(2)}) collective-permute-start(bf16[2,128,512]{2,1,0:T(8,128)(2,1)S(1)} %pad_maximum_fusion.w0), channel_id=1, source_target_pairs={{0,3},{1,4},{2,5},{3,6},{4,7},{5,8},{6,9},{7,10},{8,11},{9,12},{10... | collective-permute-start | bytes 786440 | tf_op jit(solution)/shard_map/ppermute | solution.py:299
  86.3 0.0 collective-permute-done.4.w1
  86.3 3.7 %collective-permute-done.3.w2 = bf16[2,128,512]{2,1,0:T(8,128)(2,1)} collective-permute-done((bf16[2,128,512]{2,1,0:T(8,128)(2,1)S(1)}, bf16[2,128,512]{2,1,0:T(8,128)(2,1)}, u32[]{:S(2)}, u32[]{:S(2)}) %collective-permute-start.3) | collective-permute-done | bytes 262176 | tf_op jit(solution)/shard_map/ppermute | solution.py:299
  90.0 5.6 %collective-permute-done.2.w3 = bf16[2,128,512]{2,1,0:T(8,128)(2,1)} collective-permute-done((bf16[2,128,512]{2,1,0:T(8,128)(2,1)S(1)}, bf16[2,128,512]{2,1,0:T(8,128)(2,1)}, u32[]{:S(2)}, u32[]{:S(2)}) %collective-permute-start.2) | collective-permute-done | bytes 262176 | tf_op jit(solution)/shard_map/ppermute | solution.py:299
  95.6 0.0 copy-done.3
  95.6 0.0 copy-done.5
  95.6 0.0 copy-start.4
  95.6 1.2 copy-done.4
  96.9 0.0 copy-start.2
  96.9 11.9 %shard_map.112 = (bf16[2,128,512]{2,1,0:T(8,128)(2,1)S(1)}, bf16[2,128,512]{2,1,0:T(8,128)(2,1)S(1)}, bf16[2,128,512]{2,1,0:T(8,128)(2,1)S(1)}, f32[2,128,512]{2,1,0:T(8,128)S(1)}) custom-call(s32[1]{0:T(128)} %bitcast.base, s32[32]{0:T(128)S(1)} %bitcast.33, bf16[1,128,4096]{2,1,0:T(8,128)(2,1)S(1)} %copy-done.3, bf16[1,128,4096]{2,1,0:T(8,128)(2,1)S(1)} %copy-done.4, ...), custom_call_target="tpu_custom_call" | custom-call | tf_op jit(solution)/shard_map/pallas_call | solution.py:136
  108.7 1.3 collective-permute-start.5
  110.0 1.3 collective-permute-start.6
  111.3 1.3 collective-permute-start.7
  112.6 14.7 %collective-permute-done.5 = bf16[2,128,512]{2,1,0:T(8,128)(2,1)S(1)} collective-permute-done((bf16[2,128,512]{2,1,0:T(8,128)(2,1)S(1)}, bf16[2,128,512]{2,1,0:T(8,128)(2,1)S(1)}, u32[]{:S(2)}, u32[]{:S(2)}) %collective-permute-start.5) | collective-permute-done | bytes 262176 | tf_op jit(solution)/shard_map/ppermute | solution.py:304
  127.4 12.1 %collective-permute-done.6 = bf16[2,128,512]{2,1,0:T(8,128)(2,1)S(1)} collective-permute-done((bf16[2,128,512]{2,1,0:T(8,128)(2,1)S(1)}, bf16[2,128,512]{2,1,0:T(8,128)(2,1)S(1)}, u32[]{:S(2)}, u32[]{:S(2)}) %collective-permute-start.6) | collective-permute-done | bytes 262176 | tf_op jit(solution)/shard_map/ppermute | solution.py:304
  139.4 0.0 collective-permute-done.7
  139.4 0.1 add_convert_fusion
  139.6 2.9 %collective-permute-start.8 = (bf16[128,512]{1,0:T(8,128)(2,1)S(1)}, bf16[128,512]{1,0:T(8,128)(2,1)S(1)}, u32[]{:S(2)}, u32[]{:S(2)}) collective-permute-start(bf16[128,512]{1,0:T(8,128)(2,1)S(1)} %get-tuple-element.30), channel_id=1, source_target_pairs={{0,32},{32,0},{1,33},{33,1},{2,34},{34,2},{3,35},{35,3},{4,36},{36... | collective-permute-start | bytes 393224 | tf_op jit(solution)/shard_map/ppermute | solution.py:307
  142.5 1.0 collective-permute-done.8.refs_9_
  143.5 0.0 copy-done.2
  143.5 6.3 %shard_map.113 = (bf16[4,128,2048]{2,1,0:T(8,128)(2,1)S(1)}, f32[8,128]{1,0:T(8,128)S(1)}) custom-call(f32[64]{0:T(128)S(1)} %reshape.30.mix, bf16[1,128,8192]{2,1,0:T(8,128)(2,1)S(1)} %copy-done, bf16[1,128,8192]{2,1,0:T(8,128)(2,1)S(1)} %copy-done, bf16[1,128,8192]{2,1,0:T(8,128)(2,1)S(1)} %copy-done, bf16[1,128,8192]{2,1,0:T(8,128)(2,1)S(1)} %copy-done, ...), custom_call_target="tpu_custom_call" | custom-call | tf_op jit(solution)/shard_map/pallas_call | solution.py:198
  149.8 28.6 %all_to_all.25.terms = bf16[4,128,2048]{2,1,0:T(8,128)(2,1)S(1)} all-to-all(bf16[4,128,2048]{2,1,0:T(8,128)(2,1)S(1)} %get-tuple-element.18), channel_id=1, replica_groups=mesh['zh'=2,'x'=4,'c'=2,'y'=8,'zl'=4] {'x'}, dimensions={0} | all-to-all | bytes 4194304 | tf_op jit(solution)/shard_map/all_to_all | solution.py:310
  178.4 0.4 shard_map.114
  178.7 35.0 %all_to_all.26.blocks = bf16[32,80,128]{2,1,0:T(8,128)(2,1)S(1)} all-to-all(bf16[32,80,128]{2,1,0:T(8,128)(2,1)S(1)} %shard_map.114), channel_id=1, replica_groups=mesh['zh'=2,'x'=4,'c'=2,'y'=8,'zl'=4] {'y','zl'}, dimensions={0} | all-to-all | bytes 1310720 | tf_op jit(solution)/shard_map/all_to_all | solution.py:311
  213.7 0.2 shard_map.115
  213.9 23.3 %all_to_all.27 = bf16[16,80,128]{2,1,0:T(8,128)(2,1)S(1)} all-to-all(bf16[16,80,128]{2,1,0:T(8,128)(2,1)S(1)} %shard_map.115), channel_id=1, replica_groups=mesh['zh'=2,'x'=4,'c'=2,'y'=8,'zl'=4] {'zh','x','c'}, dimensions={0} | all-to-all | bytes 655360 | tf_op jit(solution)/shard_map/all_to_all | solution.py:312
  237.3 0.1 slice_add_fusion
  237.4 0.7 copy.17
  238.2 0.7 squeeze.35
  238.9 0.7 squeeze.34
  239.6 0.7 copy.16
  (11 shorter events, 0.2 us)
Async XLA Ops:
  2.5 30.0 %all-to-all-start = ((bf16[32,64,128]{2,1,0:T(8,128)(2,1)}), bf16[32,64,128]{2,1,0:T(8,128)(2,1)S(1)}, u32[]{:S(2)}, u32[]{:S(2)}) async-start(bf16[32,64,128]{2,1,0:T(8,128)(2,1)} %broadcast_in_dim.16), calls=%async_computation | async-start | bytes 1048576 | tf_op jit(solution)/shard_map/all_to_all | solution.py:288
  16.0 23.0 %collective-permute-start = (bf16[1,128,8192]{2,1,0:T(8,128)(2,1)}, bf16[1,128,8192]{2,1,0:T(8,128)(2,1)}, u32[]{:S(2)}, u32[]{:S(2)}) collective-permute-start(bf16[1,128,8192]{2,1,0:T(8,128)(2,1)} %refs_3_.1), channel_id=1, source_target_pairs={{0,32},{32,0},{1,33},{33,1},{2,34},{34,2},{3,35},{35,3},{4,36},{36... | collective-permute-start | bytes 6291464 | tf_op jit(solution)/shard_map/ppermute | solution.py:282
  34.2 4.6 %copy-start.6 = (f32[4,4,4]{2,1,0:T(4,128)S(1)}, f32[4,4,4]{2,1,0:T(4,128)}, u32[]{:S(2)}) copy-start(f32[4,4,4]{2,1,0:T(4,128)} %param.14) | copy-start | bytes 772
  34.2 4.6 %copy-start.7 = (f32[4,4,4]{2,1,0:T(4,128)S(1)}, f32[4,4,4]{2,1,0:T(4,128)}, u32[]{:S(2)}) copy-start(f32[4,4,4]{2,1,0:T(4,128)} %param.15) | copy-start | bytes 772
  34.2 28.3 %copy-start = (bf16[1,128,8192]{2,1,0:T(8,128)(2,1)S(1)}, bf16[1,128,8192]{2,1,0:T(8,128)(2,1)}, u32[]{:S(2)}) copy-start(bf16[1,128,8192]{2,1,0:T(8,128)(2,1)} %refs_3_.1) | copy-start | bytes 6291460
  34.2 28.3 %all-to-all-start.1 = ((bf16[4,2048,128]{2,1,0:T(8,128)(2,1)}), bf16[4,2048,128]{2,1,0:T(8,128)(2,1)}, u32[]{:S(2)}, u32[]{:S(2)}) async-start(bf16[4,2048,128]{2,1,0:T(8,128)(2,1)} %broadcast_in_dim.18), calls=%async_computation.1 | async-start | bytes 4194304 | tf_op jit(solution)/shard_map/all_to_all | solution.py:289
  38.9 56.7 %copy-start.3 = (bf16[1,128,4096]{2,1,0:T(8,128)(2,1)S(1)}, bf16[1,128,4096]{2,1,0:T(8,128)(2,1)}, u32[]{:S(2)}) copy-start(bf16[1,128,4096]{2,1,0:T(8,128)(2,1)} %q.1) | copy-start | bytes 3145732
  39.0 56.7 %copy-start.5 = (s32[1,32]{1,0:T(1,128)S(1)}, s32[1,32]{1,0:T(1,128)}, u32[]{:S(2)}) copy-start(s32[1,32]{1,0:T(1,128)} %param.11) | copy-start | bytes 388
  68.4 1.3 copy-start.1
  69.8 6.5 %collective-permute-start.1 = (bf16[128,512]{1,0:T(8,128)(2,1)S(1)}, bf16[128,512]{1,0:T(8,128)(2,1)S(1)}, u32[]{:S(2)}, u32[]{:S(2)}) collective-permute-start(bf16[128,512]{1,0:T(8,128)(2,1)S(1)} %slice_bitcast_fusion.3), channel_id=1, source_target_pairs={{0,32},{32,0},{1,33},{33,1},{2,34},{34,2},{3,35},{35,3},{4,36},{36... | collective-permute-start | bytes 393224 | tf_op jit(solution)/shard_map/ppermute | solution.py:294
  76.3 10.0 %collective-permute-start.4 = (bf16[2,128,512]{2,1,0:T(8,128)(2,1)S(1)}, bf16[2,128,512]{2,1,0:T(8,128)(2,1)}, u32[]{:S(2)}, u32[]{:S(2)}) collective-permute-start(bf16[2,128,512]{2,1,0:T(8,128)(2,1)S(1)} %pad_maximum_fusion.w0), channel_id=1, source_target_pairs={{0,1},{1,2},{2,3},{3,4},{4,5},{5,6},{6,7},{7,8},{8,9},{9,10},{10,1... | collective-permute-start | bytes 786440 | tf_op jit(solution)/shard_map/ppermute | solution.py:299
  79.7 10.3 %collective-permute-start.3 = (bf16[2,128,512]{2,1,0:T(8,128)(2,1)S(1)}, bf16[2,128,512]{2,1,0:T(8,128)(2,1)}, u32[]{:S(2)}, u32[]{:S(2)}) collective-permute-start(bf16[2,128,512]{2,1,0:T(8,128)(2,1)S(1)} %pad_maximum_fusion.w0), channel_id=1, source_target_pairs={{0,2},{1,3},{2,4},{3,5},{4,6},{5,7},{6,8},{7,9},{8,10},{9,11},{10,... | collective-permute-start | bytes 786440 | tf_op jit(solution)/shard_map/ppermute | solution.py:299
  83.4 12.2 %collective-permute-start.2 = (bf16[2,128,512]{2,1,0:T(8,128)(2,1)S(1)}, bf16[2,128,512]{2,1,0:T(8,128)(2,1)}, u32[]{:S(2)}, u32[]{:S(2)}) collective-permute-start(bf16[2,128,512]{2,1,0:T(8,128)(2,1)S(1)} %pad_maximum_fusion.w0), channel_id=1, source_target_pairs={{0,3},{1,4},{2,5},{3,6},{4,7},{5,8},{6,9},{7,10},{8,11},{9,12},{10... | collective-permute-start | bytes 786440 | tf_op jit(solution)/shard_map/ppermute | solution.py:299
  95.6 1.2 copy-start.4
  96.9 46.6 %copy-start.2 = (f32[4,256,512]{2,1,0:T(8,128)S(1)}, f32[4,256,512]{2,1,0:T(8,128)}, u32[]{:S(2)}) copy-start(f32[4,256,512]{2,1,0:T(8,128)} %copy-done.1) | copy-start | bytes 6291460
  108.7 18.6 %collective-permute-start.5 = (bf16[2,128,512]{2,1,0:T(8,128)(2,1)S(1)}, bf16[2,128,512]{2,1,0:T(8,128)(2,1)S(1)}, u32[]{:S(2)}, u32[]{:S(2)}) collective-permute-start(bf16[2,128,512]{2,1,0:T(8,128)(2,1)S(1)} %get-tuple-element.14), channel_id=1, source_target_pairs={{3,0},{4,1},{5,2},{6,3},{7,4},{8,5},{9,6},{10,7},{11,8},{12,9},{13... | collective-permute-start | bytes 786440 | tf_op jit(solution)/shard_map/ppermute | solution.py:304
  110.0 29.4 %collective-permute-start.6 = (bf16[2,128,512]{2,1,0:T(8,128)(2,1)S(1)}, bf16[2,128,512]{2,1,0:T(8,128)(2,1)S(1)}, u32[]{:S(2)}, u32[]{:S(2)}) collective-permute-start(bf16[2,128,512]{2,1,0:T(8,128)(2,1)S(1)} %get-tuple-element.15), channel_id=1, source_target_pairs={{2,0},{3,1},{4,2},{5,3},{6,4},{7,5},{8,6},{9,7},{10,8},{11,9},{12,... | collective-permute-start | bytes 786440 | tf_op jit(solution)/shard_map/ppermute | solution.py:304
  111.3 28.1 %collective-permute-start.7 = (bf16[2,128,512]{2,1,0:T(8,128)(2,1)S(1)}, bf16[2,128,512]{2,1,0:T(8,128)(2,1)S(1)}, u32[]{:S(2)}, u32[]{:S(2)}) collective-permute-start(bf16[2,128,512]{2,1,0:T(8,128)(2,1)S(1)} %get-tuple-element.16), channel_id=1, source_target_pairs={{1,0},{2,1},{3,2},{4,3},{5,4},{6,5},{7,6},{8,7},{9,8},{10,9},{11,1... | collective-permute-start | bytes 786440 | tf_op jit(solution)/shard_map/ppermute | solution.py:304
  139.6 3.9 %collective-permute-start.8 = (bf16[128,512]{1,0:T(8,128)(2,1)S(1)}, bf16[128,512]{1,0:T(8,128)(2,1)S(1)}, u32[]{:S(2)}, u32[]{:S(2)}) collective-permute-start(bf16[128,512]{1,0:T(8,128)(2,1)S(1)} %get-tuple-element.30), channel_id=1, source_target_pairs={{0,32},{32,0},{1,33},{33,1},{2,34},{34,2},{3,35},{35,3},{4,36},{36... | collective-permute-start | bytes 393224 | tf_op jit(solution)/shard_map/ppermute | solution.py:307

commit v2 on v1

v2 whole, which is shorter than its diff:
```python
import functools
import math

import jax
import jax.numpy as jnp
from jax import lax
from jax.experimental import pallas as pl
from jax.experimental.pallas import tpu as pltpu
from jax.sharding import Mesh, PartitionSpec as P

KVH = 4
HD = 128
REACH = 3
GROUP = 8
NPHM = 4
PAD = 16
CTX = ("y", "zl")
DP = ("zh", "x", "c")
SCALE = 1.0 / math.sqrt(HD)
LOG2E = 1.4426950408889634
SMEM = pl.BlockSpec(memory_space=pltpu.SMEM)
F32 = jnp.float32
BF16 = jnp.bfloat16


def dot(a, b, ca, cb):
    return lax.dot_general(a, b, (((ca,), (cb,)), ((), ())), preferred_element_type=F32)


def around(distance):
    return [(i, (i + distance) % NPHM) for i in range(NPHM)]


def params(mib):
    return pltpu.CompilerParams(vmem_limit_bytes=mib << 20)


def project_kernel(mix, xm, xo, w, part, out, wide, acc):
    a = pl.program_id(0)

    @pl.when(a == 0)
    def _():
        for i in range(NPHM):
            wide[:, i * HD : (i + 1) * HD] = w[i]
        acc[...] = jnp.zeros_like(acc)

    x = jnp.concatenate([xm[0], xo[0]], axis=0)
    one = dot(x, wide[...], 1, 0)
    part[0] = one
    for b in range(NPHM):
        at = slice(b * HD, (b + 1) * HD)
        total = acc[:, at]
        for i in range(NPHM):
            total = total + mix[i * 16 + a * 4 + b] * one[:, i * HD : (i + 1) * HD]
        acc[:, at] = total

    @pl.when(a == NPHM - 1)
    def _():
        tok = xm.shape[1]
        for b in range(NPHM):
            done = acc[:, b * HD : (b + 1) * HD].astype(BF16)
            out[0, b] = done[:tok]
            out[1, b] = done[tok:]


def project(mix, xm, xo, w):
    tok, width = xm.shape[1:]
    dq, cols = width // NPHM, NPHM * HD
    return pl.pallas_call(
        project_kernel,
        grid=(NPHM,),
        in_specs=[
            SMEM,
            pl.BlockSpec((1, tok, dq), lambda a: (0, 0, a)),
            pl.BlockSpec((1, tok, dq), lambda a: (0, 0, a)),
            pl.BlockSpec((NPHM, dq, HD), lambda a: (0, 0, 0)),
        ],
        out_specs=[
            pl.BlockSpec((1, 2 * tok, cols), lambda a: (a, 0, 0)),
            pl.BlockSpec((2, NPHM, tok, HD), lambda a: (0, 0, 0, 0)),
        ],
        out_shape=[
            jax.ShapeDtypeStruct((NPHM, 2 * tok, cols), F32),
            jax.ShapeDtypeStruct((2, NPHM, tok, HD), BF16),
        ],
        scratch_shapes=[pltpu.VMEM((dq, cols), BF16), pltpu.VMEM((2 * tok, cols), F32)],
        compiler_params=params(40),
    )(mix, xm, xo, w)


def attend_kernel(
    where, lens, q0, q1, q2, q3, row, before, back, own, qd, keys, values, gk, gv, bias, probs, dscores
):
    tok = q0.shape[1]
    win = (REACH + 1) * tok
    o = pl.program_id(0)

    @pl.when(o == 0)
    def _():
        for n in range(REACH):
            keys[n * tok : (n + 1) * tok] = before[n, 0]
            values[n * tok : (n + 1) * tok] = before[n, 1]
        for n in range(KVH):
            at = slice((REACH + n) * tok, (REACH + n + 1) * tok)
            keys[at] = row[n, 0]
            values[at] = row[n, 1]
        gk[...] = jnp.zeros_like(gk)
        gv[...] = jnp.zeros_like(gv)

    for n, block in enumerate((q0, q1, q2, q3)):

        @pl.when(o == n)
        def _(block=block):
            qd[...] = block[...]

    run = (where[1] + KVH - o) & (KVH - 1)
    start = (where[0] * KVH + run) * tok
    qpos = start + lax.broadcasted_iota(jnp.int32, (8, tok), 1)

    def step(n, carry):
        end, first = carry
        end = end + lens[n]
        return end, jnp.where(end <= qpos, end, first)

    _, first = lax.fori_loop(
        0, lens.shape[0], step, (jnp.int32(0), jnp.zeros((8, tok), jnp.int32))
    )
    kpos = start - REACH * tok + lax.broadcasted_iota(jnp.int32, (win, tok), 0)
    ok = (kpos >= first[0:1]) & (kpos <= qpos[0:1])
    bias[...] = jnp.where(ok, 0.0, -1e30).astype(F32)

    here = pl.ds(pl.multiple_of(run * tok, tok), win)
    k = keys[here, :]
    v = values[here, :]
    for r in range(GROUP):
        at = slice(r * HD, (r + 1) * HD)
        rows = slice(r * tok, (r + 1) * tok)
        s = dot(k, qd[0, :, at], 1, 1) * (SCALE * LOG2E) + bias[...]
        dp = dot(v, qd[1, :, at], 1, 1)
        e = jnp.exp2(s - jnp.max(s, axis=0, keepdims=True))
        p = e * (1.0 / jnp.sum(e, axis=0, keepdims=True))
        delta = jnp.sum(p * dp, axis=0, keepdims=True)
        probs[:, rows] = p.astype(BF16)
        dscores[:, rows] = (p * (dp - delta)).astype(BF16)
    qs = jnp.concatenate([qd[0, :, r * HD : (r + 1) * HD] for r in range(GROUP)], axis=0)
    dos = jnp.concatenate([qd[1, :, r * HD : (r + 1) * HD] for r in range(GROUP)], axis=0)
    gk[here, :] = gk[here, :] + dot(dscores[...], qs, 1, 0) * SCALE
    gv[here, :] = gv[here, :] + dot(probs[...], dos, 1, 0)

    @pl.when(o == KVH - 1)
    def _():
        for n in range(REACH):
            back[n, 0] = gk[n * tok : (n + 1) * tok].astype(BF16)
            back[n, 1] = gv[n * tok : (n + 1) * tok].astype(BF16)
        for n in range(KVH):
            at = slice((REACH + n) * tok, (REACH + n + 1) * tok)
            own[n, 0] = gk[at]
            own[n, 1] = gv[at]


def attend(where, lens, qs, row, before):
    tok = row.shape[2]
    win, span = (REACH + 1) * tok, (REACH + KVH) * tok
    wide = GROUP * HD

    def whole(*shape):
        return pl.BlockSpec(shape, lambda o: (0,) * len(shape))

    return pl.pallas_call(
        attend_kernel,
        grid=(KVH,),
        in_specs=[SMEM, SMEM]
        + [whole(2, tok, wide)] * KVH
        + [whole(KVH, 2, tok, HD), whole(REACH, 2, tok, HD)],
        out_specs=[whole(REACH, 2, tok, HD), whole(KVH, 2, tok, HD)],
        out_shape=[
            jax.ShapeDtypeStruct((REACH, 2, tok, HD), BF16),
            jax.ShapeDtypeStruct((KVH, 2, tok, HD), F32),
        ],
        scratch_shapes=[
            pltpu.VMEM((2, tok, wide), BF16),
            pltpu.VMEM((span, HD), BF16),
            pltpu.VMEM((span, HD), BF16),
            pltpu.VMEM((span, HD), F32),
            pltpu.VMEM((span, HD), F32),
            pltpu.VMEM((win, tok), F32),
            pltpu.VMEM((win, GROUP * tok), BF16),
            pltpu.VMEM((win, GROUP * tok), BF16),
        ],
        compiler_params=params(40),
    )(where, lens, *qs, row, before)


def mixing_line(part, grads):
    sums = []
    for i in range(NPHM):
        for a in range(NPHM):
            for b in range(NPHM):
                both = part[a, :, i * HD : (i + 1) * HD] * grads[:, b * HD : (b + 1) * HD]
                sums.append(jnp.sum(both, axis=0, keepdims=True))
    sums = jnp.sum(jnp.concatenate(sums, axis=0), axis=1, keepdims=True)
    many = NPHM**3
    spot = lax.broadcasted_iota(jnp.int32, (many, HD), 0)
    lane = lax.broadcasted_iota(jnp.int32, (many, HD), 1)
    return jnp.sum(jnp.where(spot == lane, sums, 0.0), axis=0, keepdims=True)


def factor_kernel(which, mix, *refs):
    xs, (gm, go), refs = refs[:8], refs[8:10], refs[10:]
    (mixed, grads), refs = refs[-2:], refs[:-2]
    j = pl.program_id(0)
    tok = gm.shape[1]

    @pl.when(j == 0)
    def _():
        for b in range(NPHM):
            grads[:tok, b * HD : (b + 1) * HD] = gm[b].astype(F32)
            grads[tok:, b * HD : (b + 1) * HD] = go[b].astype(F32)
        for a in range(NPHM):
            for n, i in enumerate(which):
                total = mix[i * 16 + a * 4] * grads[:, :HD]
                for b in range(1, NPHM):
                    total = total + mix[i * 16 + a * 4 + b] * grads[:, b * HD : (b + 1) * HD]
                mixed[a, :, n * HD : (n + 1) * HD] = total.astype(BF16)
        if 0 in which:
            row = refs[-1]
            row[...] = jnp.broadcast_to(mixing_line(refs[0], grads), row.shape)

    total = None
    for a in range(NPHM):
        x = jnp.concatenate([xs[a][0], xs[4 + a][0]], axis=0)
        one = dot(mixed[a], x, 0, 0)
        total = one if total is None else total + one
    outs = refs[1:3] if 0 in which else refs[:2]
    for n, out in enumerate(outs):
        out[...] = total[n * HD : (n + 1) * HD].astype(BF16)


def factor_grads(which, mix, xm, xo, gm, go, part=None):
    tok, width = xm.shape[1:]
    dq, cols = width // NPHM, NPHM * HD
    steps = 4
    wide = dq // steps
    xspecs = [
        pl.BlockSpec((1, tok, wide), functools.partial(lambda a, j: (0, 0, a * steps + j), a))
        for a in range(NPHM)
    ]
    whole = pl.BlockSpec((NPHM, tok, HD), lambda j: (0, 0, 0))
    ins = [SMEM] + xspecs + xspecs + [whole, whole]
    args = [mix] + [xm] * 4 + [xo] * 4 + [gm, go]
    out_specs = [pl.BlockSpec((HD, wide), lambda j: (0, j))] * 2
    out_shape = [jax.ShapeDtypeStruct((HD, dq), BF16)] * 2
    if part is not None:
        ins.append(pl.BlockSpec((NPHM, 2 * tok, cols), lambda j: (0, 0, 0)))
        args.append(part)
        out_specs.append(pl.BlockSpec((8, HD), lambda j: (0, 0)))
        out_shape.append(jax.ShapeDtypeStruct((8, HD), F32))
    return pl.pallas_call(
        functools.partial(factor_kernel, which),
        grid=(steps,),
        in_specs=ins,
        out_specs=out_specs,
        out_shape=out_shape,
        scratch_shapes=[
            pltpu.VMEM((NPHM, 2 * tok, 2 * HD), BF16),
            pltpu.VMEM((2 * tok, cols), F32),
        ],
        compiler_params=params(40),
    )(*args)


def split_line(value):
    lane = lax.broadcasted_iota(jnp.int32, value.shape, 1)
    high = value.astype(BF16).astype(F32)
    return jnp.where(lane < HD // 2, high, value - high)


def turn_kernel(t0, t1, t2, t3, row, out):
    n, rows = out.shape[0], out.shape[1] - PAD
    total = t0[...].astype(F32)
    for t in (t1, t2, t3):
        total = total + t[...].astype(F32)
    turned = total.T.astype(BF16)
    line = row[0:1]
    line = line + jnp.concatenate([line[:, HD // 2 :], line[:, : HD // 2]], axis=1)
    line = jnp.broadcast_to(split_line(line), (PAD, HD)).astype(BF16)
    for d in range(n):
        out[d, :rows] = turned[d * rows : (d + 1) * rows]
        out[d, rows:] = line


def turn(terms, row, n):
    rows = terms[0].shape[1] // n
    return pl.pallas_call(
        turn_kernel,
        out_shape=jax.ShapeDtypeStruct((n, rows + PAD, HD), BF16),
        compiler_params=params(40),
    )(*terms, row)


def total_kernel(blocks, out):
    rows = out.shape[1] - PAD
    total = blocks[0].astype(F32)
    for d in range(1, blocks.shape[0]):
        total = total + blocks[d].astype(F32)
    line = total[rows : rows + 1]
    line = line + jnp.concatenate([line[:, HD // 2 :], line[:, : HD // 2]], axis=1)
    line = jnp.broadcast_to(split_line(line), (PAD, HD)).astype(BF16)
    body = total[:rows].astype(BF16)
    for d in range(out.shape[0]):
        out[d, :rows] = body
        out[d, rows:] = line


def total(blocks, n):
    return pl.pallas_call(
        total_kernel,
        out_shape=jax.ShapeDtypeStruct((n,) + blocks.shape[1:], BF16),
        compiler_params=params(40),
    )(blocks)


def final_kernel(blocks, gk, gv, mk, mv):
    half = NPHM * 2
    rows = gk.shape[0]
    lines = [None, None]
    for i in range(NPHM):
        for c, out in enumerate((gk, gv)):
            at = i * 2 + c
            block = blocks[at].astype(F32)
            for z in range(at + half, blocks.shape[0], half):
                block = block + blocks[z].astype(F32)
            out[:, i, :] = block[:rows]
            line = block[rows : rows + 1]
            lines[c] = line if lines[c] is None else lines[c] + line
    row = lax.broadcasted_iota(jnp.int32, (NPHM, HD), 0)
    lane = lax.broadcasted_iota(jnp.int32, (NPHM, HD), 1)
    col = lax.broadcasted_iota(jnp.int32, (NPHM, NPHM), 1)
    for line, out in zip(lines, (mk, mv)):
        for i in range(NPHM):
            tile = jnp.zeros((NPHM, NPHM), F32)
            for b in range(NPHM):
                mine = (lane & (HD // 2 - 1)) == i * 16 + row * 4 + b
                tile = jnp.where(col == b, jnp.sum(jnp.where(mine, line, 0.0), axis=1, keepdims=True), tile)
            out[i] = tile


def final(blocks, rows):
    return pl.pallas_call(
        final_kernel,
        out_shape=[jax.ShapeDtypeStruct((rows, NPHM, HD), F32)] * 2
        + [jax.ShapeDtypeStruct((NPHM, NPHM, NPHM), F32)] * 2,
        compiler_params=params(40),
    )(blocks)


def shards(inputs, queries, upstream, lengths, factor_k, factor_v, mixing_k, mixing_v):
    tok = inputs.shape[1]
    rows = factor_k.shape[0]
    n_ctx = lax.axis_size("y") * lax.axis_size("zl")
    n_dp = lax.axis_size("zh") * lax.axis_size("x") * lax.axis_size("c")
    z_at = lax.axis_index("zl")
    x_at = lax.axis_index("x")
    first = lax.axis_index("c") == 0
    swap = [(0, 1), (1, 0)]

    other = lax.ppermute(inputs, "c", swap)
    mix = jnp.where(first, mixing_k, mixing_v)
    turned = lax.dynamic_slice_in_dim(jnp.concatenate([mix, mix]), x_at, NPHM, 0).reshape(-1)
    mine = lax.dynamic_index_in_dim(
        jnp.where(first, factor_k, factor_v), x_at, axis=1, keepdims=False
    )
    piece = jnp.broadcast_to(mine[None], (n_ctx, rows, HD))
    wide = GROUP * HD
    blocks = []
    for o in range(KVH):
        head = ((z_at + o) & (KVH - 1)) * wide
        blocks.append(
            jnp.stack([lax.dynamic_slice_in_dim(m[0], head, wide, 1) for m in (queries, upstream)])
        )
    piece = lax.all_to_all(piece, CTX, 0, 0, tiled=True).reshape(1, n_ctx * rows, HD)
    q1 = lax.ppermute(blocks[1], "zl", around(1))
    piece, q1, b2 = lax.optimization_barrier((piece, q1, blocks[2]))
    q2 = lax.ppermute(b2, "zl", around(2))
    weights = lax.all_to_all(
        jnp.broadcast_to(piece, (NPHM, n_ctx * rows, HD)), "x", 0, 0, tiled=True
    )
    weights, q2, b3 = lax.optimization_barrier((weights, q2, blocks[3]))
    q3 = lax.ppermute(b3, "zl", around(3))
    part, both = project(mix.reshape(-1), inputs, other, weights)

    got = lax.ppermute(both[1], "c", swap)
    pack = jnp.stack([jnp.where(first, both[0], got), jnp.where(first, got, both[0])], axis=1)
    pack, q3 = lax.optimization_barrier((pack, q3))
    row = lax.all_to_all(pack, "zl", 0, 0, tiled=True)
    up = [(n, n + 1) for n in range(lax.axis_size("y") - 1)]
    before = lax.ppermute(row[KVH - REACH :], "y", up)
    where = jnp.stack([lax.axis_index("y"), z_at]).astype(jnp.int32)
    back, own = attend(where, lengths[0], [blocks[0], q1, q2, q3], row, before)
    back = lax.ppermute(back, "y", [(n, m) for m, n in up]).astype(F32)
    own = jnp.concatenate([own[: KVH - REACH], own[KVH - REACH :] + back])
    grads = lax.all_to_all(own.astype(BF16), "zl", 0, 0, tiled=True)
    keep = jnp.where(first, grads[:, 0], grads[:, 1])
    got = lax.ppermute(jnp.where(first, grads[:, 1], grads[:, 0]), "c", swap)

    one, three = factor_grads((1, 3), turned, inputs, other, keep, got)
    sent = [lax.ppermute(one, "x", around(1)), lax.ppermute(three, "x", around(3))]
    own, two, row = factor_grads((0, 2), turned, inputs, other, keep, got, part)
    sent.append(lax.ppermute(two, "x", around(2)))
    blocks = lax.all_to_all(turn([own] + sent, row, n_ctx), CTX, 0, 0, tiled=True)
    blocks = lax.all_to_all(total(blocks, n_dp), DP, 0, 0, tiled=True)
    return tuple(final(blocks, rows))


def solution(mesh):
    n_dp, n_ctx = mesh.devices.shape
    zl = 4
    shape = (n_dp // 8, 4, 2, n_ctx // zl, zl)
    wide = Mesh(mesh.devices.reshape(shape), DP + CTX)
    in_specs = (
        P(DP, CTX, None),
        P(DP, CTX, None),
        P(DP, CTX, None),
        P(DP, None),
        P(CTX, None, None),
        P(CTX, None, None),
        P(),
        P(),
    )
    out_specs = (P(CTX, None, None), P(CTX, None, None), P(), P())
    return jax.shard_map(shards, mesh=wide, in_specs=in_specs, out_specs=out_specs, check_vma=False)
```

time: 242 us -> 236 us (0.975)
  blocking collectives: 86.9 us -> 63.7 us
  starting transfers between devices: 43.2 us -> 58.2 us
  waiting for transfers between devices: 75.3 us -> 66 us
  other arithmetic: 0.37 us -> 4.75 us
  Pallas kernels: 24.6 us -> 28.7 us
    all_to_all x2, blocking collectives: 63.6 us -> 39.2 us  [the longest x1 28.1 us: shards(): lax.all_to_all(turn([own] + sent, row, n_ctx), CTX, 0, 0, tiled=True)]
    all_to_all x1, waiting for transfers between devices: 23.6 us -> 0.01 us  [shards(): lax.all_to_all(jnp.broadcast_to(piece, (NPHM, n_ctx * rows, HD)), 'x', 0,...]
    ppermute x7 -> x9, waiting for transfers between devices: 37 us -> 59.3 us  [the longest x1 21.8 us: shards(): q2 = lax.ppermute(b2, 'zl', around(2))]
    all_to_all x1, waiting for transfers between devices: 13.7 us -> 0.01 us  [shards(): lax.all_to_all(piece, CTX, 0, 0, tiled=True).reshape(1, n_ctx * rows, HD)]
    ppermute x7 -> x9, starting transfers between devices: 16.8 us -> 29.4 us  [the longest x1 6.68 us: shards(): got = lax.ppermute(jnp.where(first, grads[:, 1], grads[:, 0]), 'c', swap)]
    all_to_all x0 -> x1, waiting for transfers between devices: none -> 5.69 us  [shards(): row = lax.all_to_all(pack, 'zl', 0, 0, tiled=True)]
    another operation x2 -> x8, other arithmetic: 0.05 us -> 4.66 us  [the longest x4 3.78 us: shards(): jnp.stack([lax.dynamic_slice_in_dim(m[0], head, wide, 1) for m in (querie...]
    pallas_call x2 -> x4, Pallas kernels: 18.2 us -> 22.3 us  [the longest x1 12.1 us: attend(): pl.pallas_call(attend_kernel, grid=(KVH,), in_specs=[SMEM, SMEM] + [whole...]
  transfers between devices with their start and end apart: 11 -> 14, of which waited for: 8 -> 9; matrix products, arithmetic and copies ran while one was open for 1% -> 4% of each run, Pallas kernels for 0% -> 4%
where the time goes in v2:
time: 236 us; the launch traced here: 233 us
  waiting for transfers between devices  66 us (28%)
  blocking collectives  63.7 us (27%)
  starting transfers between devices  58.2 us (25%)
  Pallas kernels  28.7 us (12%)
  local copies, waits for them, and re-layouts  11.3 us (5%)
  other arithmetic  4.75 us (2%)
    all_to_all x1, blocking collectives, shards(): lax.all_to_all(turn([own] + sent, row, n_ctx), CTX, 0, 0, tiled=True)  28.1 us
    all_to_all x1, blocking collectives, shards(): blocks = lax.all_to_all(total(blocks, n_dp), DP, 0, 0, tiled=True)  24.5 us
    ppermute x1, waiting for transfers between devices, shards(): q2 = lax.ppermute(b2, 'zl', around(2))  21.8 us
    ppermute x1, waiting for transfers between devices, shards(): q1 = lax.ppermute(blocks[1], 'zl', around(1))  16.9 us
    all_to_all x1, starting transfers between devices, shards(): lax.all_to_all(piece, CTX, 0, 0, tiled=True).reshape(1, n_ctx * rows, HD)  13.5 us
    pallas_call x1, Pallas kernels, attend(): pl.pallas_call(attend_kernel, grid=(KVH,), in_specs=[SMEM, SMEM] + [whole...  12.1 us
    ppermute x1, waiting for transfers between devices, shards(): lax.ppermute(one, 'x', around(1))  11.6 us
    all_to_all x1, blocking collectives, shards(): grads = lax.all_to_all(own.astype(BF16), 'zl', 0, 0, tiled=True)  11.1 us
  transfers between devices with their start and end apart: 14, of which 9 were waited for; matrix products, arithmetic and copies ran while one was open for 4% of the time, Pallas kernels for 4%

profile of v2, /device:TPU:1, one launch (start us, length us, event | category | flops | bytes accessed | tf_op | source)
XLA Modules:
  0.0 233.5 jit_solution(7231416376991529402)
XLA Ops:
  0.6 1.0 constant_dynamic-slice_fusion.6
  1.6 0.9 broadcast_in_dim.16
  2.5 13.5 %all-to-all-start = ((bf16[32,64,128]{2,1,0:T(8,128)(2,1)}), bf16[32,64,128]{2,1,0:T(8,128)(2,1)S(1)}, u32[]{:S(2)}, u32[]{:S(2)}) async-start(bf16[32,64,128]{2,1,0:T(8,128)(2,1)} %broadcast_in_dim.16), calls=%async_computation | async-start | bytes 1048576 | tf_op jit(solution)/shard_map/all_to_all | solution.py:381
  16.0 0.0 copy-start
  16.0 2.7 %constant_dynamic-slice_fusion = (bf16[1,128,1024]{2,1,0:T(8,128)(2,1)S(1)}, bf16[1,128,1024]{2,1,0:T(8,128)(2,1)S(1)}, bf16[1,128,1024]{2,1,0:T(8,128)(2,1)}, b...) fusion(bf16[1,128,4096]{2,1,0:T(8,128)(2,1)} %param.10, ...), kind=kLoop, calls=%fused_computation.23 | loop fusion | bytes 4194320 | tf_op jit(solution)/shard_map/dynamic_slice | solution.py:379
  18.8 0.1 pad_maximum_fusion.1
  18.8 3.1 %collective-permute-start.1 = (bf16[2,128,1024]{2,1,0:T(8,128)(2,1)S(1)}, bf16[2,128,1024]{2,1,0:T(8,128)(2,1)S(1)}, u32[]{:S(2)}, u32[]{:S(2)}) collective-permute-start(bf16[2,128,1024]{2,1,0:T(8,128)(2,1)S(1)} %pad_maximum_fusion.1), channel_id=1, source_target_pairs={{0,1},{1,2},{2,3},{3,0},{4,5},{5,6},{6,7},{7,4},{8,9},{9,10},{10,1... | collective-permute-start | bytes 1572872 | tf_op jit(solution)/shard_map/ppermute | solution.py:382
  22.0 0.0 copy-done
  22.0 3.4 %collective-permute-start = (bf16[1,128,8192]{2,1,0:T(8,128)(2,1)S(1)}, bf16[1,128,8192]{2,1,0:T(8,128)(2,1)}, u32[]{:S(2)}, u32[]{:S(2)}) collective-permute-start(bf16[1,128,8192]{2,1,0:T(8,128)(2,1)S(1)} %copy-done), channel_id=1, source_target_pairs={{0,32},{32,0},{1,33},{33,1},{2,34},{34,2},{3,35},{35,3},{4,36},{36... | collective-permute-start | bytes 6291464 | tf_op jit(solution)/shard_map/ppermute | solution.py:367
  25.4 0.8 pad_maximum_fusion.2
  26.2 16.9 %collective-permute-done.1.q1 = bf16[2,128,1024]{2,1,0:T(8,128)(2,1)S(1)} collective-permute-done((bf16[2,128,1024]{2,1,0:T(8,128)(2,1)S(1)}, bf16[2,128,1024]{2,1,0:T(8,128)(2,1)S(1)}, u32[]{:S(2)}, u32[]{:S(2)}) %collective-permute-start.1) | collective-permute-done | bytes 524320 | tf_op jit(solution)/shard_map/ppermute | solution.py:382
  43.1 0.0 all-to-all-done
  43.1 1.6 broadcast_in_dim.18
  44.8 0.0 copy-start.6
  44.8 0.0 copy-start.7
  44.8 4.6 %all-to-all-start.1 = ((bf16[4,2048,128]{2,1,0:T(8,128)(2,1)}), bf16[4,2048,128]{2,1,0:T(8,128)(2,1)}, u32[]{:S(2)}, u32[]{:S(2)}) async-start(bf16[4,2048,128]{2,1,0:T(8,128)(2,1)} %broadcast_in_dim.18), calls=%async_computation.1 | async-start | bytes 4194304 | tf_op jit(solution)/shard_map/all_to_all | solution.py:385
  49.4 1.9 collective-permute-start.2
  51.3 0.0 copy-done.6
  51.3 0.0 copy-done.7
  51.4 0.1 reshape.41.mix
  51.4 1.8 pad_maximum_fusion.3
  53.3 21.8 %collective-permute-done.2.q2 = bf16[2,128,1024]{2,1,0:T(8,128)(2,1)S(1)} collective-permute-done((bf16[2,128,1024]{2,1,0:T(8,128)(2,1)}, bf16[2,128,1024]{2,1,0:T(8,128)(2,1)S(1)}, u32[]{:S(2)}, u32[]{:S(2)}) %collective-permute-start.2) | collective-permute-done | bytes 524320 | tf_op jit(solution)/shard_map/ppermute | solution.py:384
  75.1 0.0 all-to-all-done.1.w
  75.1 2.4 %collective-permute-start.4 = (bf16[2,128,1024]{2,1,0:T(8,128)(2,1)}, bf16[2,128,1024]{2,1,0:T(8,128)(2,1)S(1)}, u32[]{:S(2)}, u32[]{:S(2)}) collective-permute-start(bf16[2,128,1024]{2,1,0:T(8,128)(2,1)} %pad_maximum_fusion.3), channel_id=1, source_target_pairs={{0,3},{1,0},{2,1},{3,2},{4,7},{5,4},{6,5},{7,6},{8,11},{9,8},{10,9... | collective-permute-start | bytes 1572872 | tf_op jit(solution)/shard_map/ppermute | solution.py:389
  77.4 0.0 collective-permute-done.xo.refs_4_.refs_5_.refs_6_.refs_7_
  77.4 5.9 %shard_map.111 = (f32[4,256,512]{2,1,0:T(8,128)S(1)}, bf16[2,4,128,128]{3,2,1,0:T(8,128)(2,1)S(1)}) custom-call(f32[64]{0:T(128)S(1)} %reshape.41.mix, bf16[1,128,8192]{2,1,0:T(8,128)(2,1)S(1)} %copy-done, bf16[1,128,8192]{2,1,0:T(8,128)(2,1)} %collective-permute-done.xo.refs_4_.refs_5_.refs_6_.refs_7_, bf16[4,2048,128]{2,1,0:T(8,128)(2,1)} %all-to-all-done.1.w), custom_call_target="tpu_custom_call" | custom-call | tf_op jit(solution)/shard_map/pallas_call | solution.py:69
  83.3 0.0 copy-start.1
  83.3 1.3 copy-done.1
  84.7 0.0 copy-start.5
  84.7 3.9 %collective-permute-start.3 = (bf16[4,128,128]{2,1,0:T(8,128)(2,1)S(1)}, bf16[4,128,128]{2,1,0:T(8,128)(2,1)S(1)}, u32[]{:S(2)}, u32[]{:S(2)}) collective-permute-start(bf16[4,128,128]{2,1,0:T(8,128)(2,1)S(1)} %slice_bitcast_fusion.2), channel_id=1, source_target_pairs={{0,32},{32,0},{1,33},{33,1},{2,34},{34,2},{3,35},{35,3},{4,36},{36... | collective-permute-start | bytes 393224 | tf_op jit(solution)/shard_map/ppermute | solution.py:392
  88.6 1.0 collective-permute-done.3
  89.6 0.7 pad_maximum_fusion.4
  90.3 0.0 collective-permute-done.4.q3
  90.3 0.8 copy-done.3
  91.1 3.4 %all-to-all-start.2 = ((bf16[4,2,128,128]{3,2,1,0:T(8,128)(2,1)}), bf16[4,2,128,128]{3,2,1,0:T(8,128)(2,1)S(1)}, u32[]{:S(2)}, u32[]{:S(2)}) async-start(bf16[4,2,128,128]{3,2,1,0:T(8,128)(2,1)} %pad_maximum_fusion.4), calls=%async_computation.2 | async-start | bytes 524288 | tf_op jit(solution)/shard_map/all_to_all | solution.py:395
  94.5 5.7 %all-to-all-done.2.row = bf16[4,2,128,128]{3,2,1,0:T(8,128)(2,1)S(1)} async-done(((bf16[4,2,128,128]{3,2,1,0:T(8,128)(2,1)}), bf16[4,2,128,128]{3,2,1,0:T(8,128)(2,1)S(1)}, u32[]{:S(2)}, u32[]{:S(2)}) %all-to-all-start.2) | async-done | bytes 262176 | tf_op jit(solution)/shard_map/all_to_all | solution.py:395
  100.2 2.3 collective-permute-start.5
  102.6 0.1 pad_add_fusion.where
  102.6 1.1 pad_maximum_fusion.q0
  103.7 1.4 collective-permute-done.5.before
  105.1 0.0 copy-done.5
  105.1 1.0 copy-done.4
  106.2 12.1 %shard_map.112 = (bf16[3,2,128,128]{3,2,1,0:T(8,128)(2,1)S(1)}, f32[4,2,128,128]{3,2,1,0:T(8,128)S(1)}) custom-call(s32[2]{0:T(128)S(1)} %pad_add_fusion.where, s32[32]{0:T(128)S(1)} %bitcast.41, bf16[2,128,1024]{2,1,0:T(8,128)(2,1)S(1)} %pad_maximum_fusion.q0, bf16[2,128,1024]{2,1,0:T(8,128)(2,1)S(1)} %collective-permute-done.1.q1, ...), custom_call_target="tpu_custom_call" | custom-call | tf_op jit(solution)/shard_map/pallas_call | solution.py:169
  118.3 1.3 collective-permute-start.6
  119.6 5.6 %collective-permute-done.6 = bf16[3,2,128,128]{3,2,1,0:T(8,128)(2,1)S(1)} collective-permute-done((bf16[3,2,128,128]{3,2,1,0:T(8,128)(2,1)S(1)}, bf16[3,2,128,128]{3,2,1,0:T(8,128)(2,1)S(1)}, u32[]{:S(2)}, u32[]{:S(2)}) %collective-permute-start.6) | collective-permute-done | bytes 196640 | tf_op jit(solution)/shard_map/ppermute | solution.py:400
  125.1 0.1 add_convert_fusion
  125.2 11.1 %all_to_all.30 = bf16[4,2,128,128]{3,2,1,0:T(8,128)(2,1)S(1)} all-to-all(bf16[4,2,128,128]{3,2,1,0:T(8,128)(2,1)S(1)} %pad_maximum_fusion.5), channel_id=1, replica_groups=mesh['zh'=2,'x'=4,'c'=2,'y'=8,'zl'=4] {'zl'}, dimensions={0} | all-to-all | bytes 524288 | tf_op jit(solution)/shard_map/all_to_all | solution.py:402
  136.4 6.7 %collective-permute-start.7 = (bf16[4,128,128]{2,1,0:T(8,128)(2,1)S(1)}, bf16[4,128,128]{2,1,0:T(8,128)(2,1)S(1)}, u32[]{:S(2)}, u32[]{:S(2)}) collective-permute-start(bf16[4,128,128]{2,1,0:T(8,128)(2,1)S(1)} %get-tuple-element.48), channel_id=1, source_target_pairs={{0,32},{32,0},{1,33},{33,1},{2,34},{34,2},{3,35},{35,3},{4,36},{36... | collective-permute-start | bytes 393224 | tf_op jit(solution)/shard_map/ppermute | solution.py:404
  143.1 0.1 reshape.39.mix
  143.2 0.8 collective-permute-done.7.refs_9_
  144.0 1.6 copy-done.2
  145.6 5.1 %shard_map.113 = (bf16[128,2048]{1,0:T(8,128)(2,1)S(1)}, bf16[128,2048]{1,0:T(8,128)(2,1)S(1)}, f32[8,128]{1,0:T(8,128)S(1)}) custom-call(f32[64]{0:T(128)S(1)} %reshape.39.mix, bf16[1,128,8192]{2,1,0:T(8,128)(2,1)S(1)} %copy-done, bf16[1,128,8192]{2,1,0:T(8,128)(2,1)S(1)} %copy-done, bf16[1,128,8192]{2,1,0:T(8,128)(2,1)S(1)} %copy-done, ...), custom_call_target="tpu_custom_call" | custom-call | tf_op jit(solution)/shard_map/pallas_call | solution.py:258
  150.7 5.2 %collective-permute-start.10 = (bf16[128,2048]{1,0:T(8,128)(2,1)S(1)}, bf16[128,2048]{1,0:T(8,128)(2,1)S(1)}, u32[]{:S(2)}, u32[]{:S(2)}) collective-permute-start(bf16[128,2048]{1,0:T(8,128)(2,1)S(1)} %get-tuple-element.36), channel_id=1, source_target_pairs={{0,128},{64,192},{128,0},{192,64},{1,129},{65,193},{129,1},{193,65... | collective-permute-start | bytes 1572872 | tf_op jit(solution)/shard_map/ppermute | solution.py:409
  155.9 4.3 %shard_map.114 = (bf16[128,2048]{1,0:T(8,128)(2,1)S(1)}, bf16[128,2048]{1,0:T(8,128)(2,1)S(1)}) custom-call(f32[64]{0:T(128)S(1)} %reshape.39.mix, bf16[1,128,8192]{2,1,0:T(8,128)(2,1)S(1)} %copy-done, bf16[1,128,8192]{2,1,0:T(8,128)(2,1)S(1)} %copy-done, bf16[1,128,8192]{2,1,0:T(8,128)(2,1)S(1)} %copy-done, bf16[1,128,8192]{2,1,0:T(8,128)(2,1)S(1)} %copy-done, ...), custom_call_target="tpu_custom_call" | custom-call | tf_op jit(solution)/shard_map/pallas_call | solution.py:258
  160.2 2.2 collective-permute-start.8
  162.4 4.3 %collective-permute-start.9 = (bf16[128,2048]{1,0:T(8,128)(2,1)S(1)}, bf16[128,2048]{1,0:T(8,128)(2,1)S(1)}, u32[]{:S(2)}, u32[]{:S(2)}) collective-permute-start(bf16[128,2048]{1,0:T(8,128)(2,1)S(1)} %get-tuple-element.35), channel_id=1, source_target_pairs={{0,192},{64,0},{128,64},{192,128},{1,193},{65,1},{129,65},{193,129... | collective-permute-start | bytes 1572872 | tf_op jit(solution)/shard_map/ppermute | solution.py:407
  166.7 1.2 collective-permute-done.10.t3
  168.0 11.6 %collective-permute-done.8.t1 = bf16[128,2048]{1,0:T(8,128)(2,1)S(1)} collective-permute-done((bf16[128,2048]{1,0:T(8,128)(2,1)S(1)}, bf16[128,2048]{1,0:T(8,128)(2,1)S(1)}, u32[]{:S(2)}, u32[]{:S(2)}) %collective-permute-start.8) | collective-permute-done | bytes 524320 | tf_op jit(solution)/shard_map/ppermute | solution.py:407
  179.5 0.0 collective-permute-done.9.t2
  179.5 0.4 shard_map.115
  179.9 28.1 %all_to_all.31.blocks = bf16[32,80,128]{2,1,0:T(8,128)(2,1)S(1)} all-to-all(bf16[32,80,128]{2,1,0:T(8,128)(2,1)S(1)} %shard_map.115), channel_id=1, replica_groups=mesh['zh'=2,'x'=4,'c'=2,'y'=8,'zl'=4] {'y','zl'}, dimensions={0} | all-to-all | bytes 1310720 | tf_op jit(solution)/shard_map/all_to_all | solution.py:410
  208.0 0.2 shard_map.116
  208.2 24.5 %all_to_all.32.blocks = bf16[16,80,128]{2,1,0:T(8,128)(2,1)S(1)} all-to-all(bf16[16,80,128]{2,1,0:T(8,128)(2,1)S(1)} %shard_map.116), channel_id=1, replica_groups=mesh['zh'=2,'x'=4,'c'=2,'y'=8,'zl'=4] {'zh','x','c'}, dimensions={0} | all-to-all | bytes 655360 | tf_op jit(solution)/shard_map/all_to_all | solution.py:411
  232.6 0.8 shard_map.117
  (12 shorter events, 0.1 us)
Async XLA Ops:
  2.5 40.6 %all-to-all-start = ((bf16[32,64,128]{2,1,0:T(8,128)(2,1)}), bf16[32,64,128]{2,1,0:T(8,128)(2,1)S(1)}, u32[]{:S(2)}, u32[]{:S(2)}) async-start(bf16[32,64,128]{2,1,0:T(8,128)(2,1)} %broadcast_in_dim.16), calls=%async_computation | async-start | bytes 1048576 | tf_op jit(solution)/shard_map/all_to_all | solution.py:381
  16.0 6.0 %copy-start = (bf16[1,128,8192]{2,1,0:T(8,128)(2,1)S(1)}, bf16[1,128,8192]{2,1,0:T(8,128)(2,1)}, u32[]{:S(2)}) copy-start(bf16[1,128,8192]{2,1,0:T(8,128)(2,1)} %refs_3_.3) | copy-start | bytes 6291460
  18.8 24.3 %collective-permute-start.1 = (bf16[2,128,1024]{2,1,0:T(8,128)(2,1)S(1)}, bf16[2,128,1024]{2,1,0:T(8,128)(2,1)S(1)}, u32[]{:S(2)}, u32[]{:S(2)}) collective-permute-start(bf16[2,128,1024]{2,1,0:T(8,128)(2,1)S(1)} %pad_maximum_fusion.1), channel_id=1, source_target_pairs={{0,1},{1,2},{2,3},{3,0},{4,5},{5,6},{6,7},{7,4},{8,9},{9,10},{10,1... | collective-permute-start | bytes 1572872 | tf_op jit(solution)/shard_map/ppermute | solution.py:382
  22.0 55.4 %collective-permute-start = (bf16[1,128,8192]{2,1,0:T(8,128)(2,1)S(1)}, bf16[1,128,8192]{2,1,0:T(8,128)(2,1)}, u32[]{:S(2)}, u32[]{:S(2)}) collective-permute-start(bf16[1,128,8192]{2,1,0:T(8,128)(2,1)S(1)} %copy-done), channel_id=1, source_target_pairs={{0,32},{32,0},{1,33},{33,1},{2,34},{34,2},{3,35},{35,3},{4,36},{36... | collective-permute-start | bytes 6291464 | tf_op jit(solution)/shard_map/ppermute | solution.py:367
  44.8 6.5 %copy-start.6 = (f32[4,4,4]{2,1,0:T(4,128)S(1)}, f32[4,4,4]{2,1,0:T(4,128)}, u32[]{:S(2)}) copy-start(f32[4,4,4]{2,1,0:T(4,128)} %param.14) | copy-start | bytes 772
  44.8 6.5 %copy-start.7 = (f32[4,4,4]{2,1,0:T(4,128)S(1)}, f32[4,4,4]{2,1,0:T(4,128)}, u32[]{:S(2)}) copy-start(f32[4,4,4]{2,1,0:T(4,128)} %param.15) | copy-start | bytes 772
  44.8 30.3 %all-to-all-start.1 = ((bf16[4,2048,128]{2,1,0:T(8,128)(2,1)}), bf16[4,2048,128]{2,1,0:T(8,128)(2,1)}, u32[]{:S(2)}, u32[]{:S(2)}) async-start(bf16[4,2048,128]{2,1,0:T(8,128)(2,1)} %broadcast_in_dim.18), calls=%async_computation.1 | async-start | bytes 4194304 | tf_op jit(solution)/shard_map/all_to_all | solution.py:385
  49.4 25.7 %collective-permute-start.2 = (bf16[2,128,1024]{2,1,0:T(8,128)(2,1)}, bf16[2,128,1024]{2,1,0:T(8,128)(2,1)S(1)}, u32[]{:S(2)}, u32[]{:S(2)}) collective-permute-start(bf16[2,128,1024]{2,1,0:T(8,128)(2,1)} %pad_maximum_fusion.2), channel_id=1, source_target_pairs={{0,2},{1,3},{2,0},{3,1},{4,6},{5,7},{6,4},{7,5},{8,10},{9,11},{10,... | collective-permute-start | bytes 1572872 | tf_op jit(solution)/shard_map/ppermute | solution.py:384
  75.1 15.3 %collective-permute-start.4 = (bf16[2,128,1024]{2,1,0:T(8,128)(2,1)}, bf16[2,128,1024]{2,1,0:T(8,128)(2,1)S(1)}, u32[]{:S(2)}, u32[]{:S(2)}) collective-permute-start(bf16[2,128,1024]{2,1,0:T(8,128)(2,1)} %pad_maximum_fusion.3), channel_id=1, source_target_pairs={{0,3},{1,0},{2,1},{3,2},{4,7},{5,4},{6,5},{7,6},{8,11},{9,8},{10,9... | collective-permute-start | bytes 1572872 | tf_op jit(solution)/shard_map/ppermute | solution.py:389
  83.3 1.3 copy-start.1
  84.7 20.5 %copy-start.5 = (s32[1,32]{1,0:T(1,128)S(1)}, s32[1,32]{1,0:T(1,128)}, u32[]{:S(2)}) copy-start(s32[1,32]{1,0:T(1,128)} %param.11) | copy-start | bytes 388
  84.7 4.9 %collective-permute-start.3 = (bf16[4,128,128]{2,1,0:T(8,128)(2,1)S(1)}, bf16[4,128,128]{2,1,0:T(8,128)(2,1)S(1)}, u32[]{:S(2)}, u32[]{:S(2)}) collective-permute-start(bf16[4,128,128]{2,1,0:T(8,128)(2,1)S(1)} %slice_bitcast_fusion.2), channel_id=1, source_target_pairs={{0,32},{32,0},{1,33},{33,1},{2,34},{34,2},{3,35},{35,3},{4,36},{36... | collective-permute-start | bytes 393224 | tf_op jit(solution)/shard_map/ppermute | solution.py:392
  90.3 0.8 copy-start.3
  91.1 9.1 %all-to-all-start.2 = ((bf16[4,2,128,128]{3,2,1,0:T(8,128)(2,1)}), bf16[4,2,128,128]{3,2,1,0:T(8,128)(2,1)S(1)}, u32[]{:S(2)}, u32[]{:S(2)}) async-start(bf16[4,2,128,128]{3,2,1,0:T(8,128)(2,1)} %pad_maximum_fusion.4), calls=%async_computation.2 | async-start | bytes 524288 | tf_op jit(solution)/shard_map/all_to_all | solution.py:395
  100.2 4.9 %collective-permute-start.5 = (bf16[3,2,128,128]{3,2,1,0:T(8,128)(2,1)S(1)}, bf16[3,2,128,128]{3,2,1,0:T(8,128)(2,1)S(1)}, u32[]{:S(2)}, u32[]{:S(2)}) collective-permute-start(bf16[3,2,128,128]{3,2,1,0:T(8,128)(2,1)S(1)} %slice.32), channel_id=1, source_target_pairs={{0,4},{4,8},{8,12},{12,16},{16,20},{20,24},{24,28},{1,5},{5,9},{9,... | collective-permute-start | bytes 589832 | tf_op jit(solution)/shard_map/ppermute | solution.py:397
  105.1 1.0 copy-start.4
  118.3 6.9 %collective-permute-start.6 = (bf16[3,2,128,128]{3,2,1,0:T(8,128)(2,1)S(1)}, bf16[3,2,128,128]{3,2,1,0:T(8,128)(2,1)S(1)}, u32[]{:S(2)}, u32[]{:S(2)}) collective-permute-start(bf16[3,2,128,128]{3,2,1,0:T(8,128)(2,1)S(1)} %get-tuple-element.31), channel_id=1, source_target_pairs={{4,0},{8,4},{12,8},{16,12},{20,16},{24,20},{28,24},{5,1},{9,5},{13... | collective-permute-start | bytes 589832 | tf_op jit(solution)/shard_map/ppermute | solution.py:400
  136.4 7.7 %collective-permute-start.7 = (bf16[4,128,128]{2,1,0:T(8,128)(2,1)S(1)}, bf16[4,128,128]{2,1,0:T(8,128)(2,1)S(1)}, u32[]{:S(2)}, u32[]{:S(2)}) collective-permute-start(bf16[4,128,128]{2,1,0:T(8,128)(2,1)S(1)} %get-tuple-element.48), channel_id=1, source_target_pairs={{0,32},{32,0},{1,33},{33,1},{2,34},{34,2},{3,35},{35,3},{4,36},{36... | collective-permute-start | bytes 393224 | tf_op jit(solution)/shard_map/ppermute | solution.py:404
  144.0 1.6 copy-start.2
  150.7 17.3 %collective-permute-start.10 = (bf16[128,2048]{1,0:T(8,128)(2,1)S(1)}, bf16[128,2048]{1,0:T(8,128)(2,1)S(1)}, u32[]{:S(2)}, u32[]{:S(2)}) collective-permute-start(bf16[128,2048]{1,0:T(8,128)(2,1)S(1)} %get-tuple-element.36), channel_id=1, source_target_pairs={{0,128},{64,192},{128,0},{192,64},{1,129},{65,193},{129,1},{193,65... | collective-permute-start | bytes 1572872 | tf_op jit(solution)/shard_map/ppermute | solution.py:409
  160.2 19.3 %collective-permute-start.8 = (bf16[128,2048]{1,0:T(8,128)(2,1)S(1)}, bf16[128,2048]{1,0:T(8,128)(2,1)S(1)}, u32[]{:S(2)}, u32[]{:S(2)}) collective-permute-start(bf16[128,2048]{1,0:T(8,128)(2,1)S(1)} %get-tuple-element.34), channel_id=1, source_target_pairs={{0,64},{64,128},{128,192},{192,0},{1,65},{65,129},{129,193},{193,1... | collective-permute-start | bytes 1572872 | tf_op jit(solution)/shard_map/ppermute | solution.py:407
  162.4 17.1 %collective-permute-start.9 = (bf16[128,2048]{1,0:T(8,128)(2,1)S(1)}, bf16[128,2048]{1,0:T(8,128)(2,1)S(1)}, u32[]{:S(2)}, u32[]{:S(2)}) collective-permute-start(bf16[128,2048]{1,0:T(8,128)(2,1)S(1)} %get-tuple-element.35), channel_id=1, source_target_pairs={{0,192},{64,0},{128,64},{192,128},{1,193},{65,1},{129,65},{193,129... | collective-permute-start | bytes 1572872 | tf_op jit(solution)/shard_map/ppermute | solution.py:407

commit v3 on v2

v3 whole, which is shorter than its diff:
```python
import functools
import math

import jax
import jax.numpy as jnp
from jax import lax
from jax.experimental import pallas as pl
from jax.experimental.pallas import tpu as pltpu
from jax.sharding import Mesh, PartitionSpec as P

KVH = 4
HD = 128
REACH = 3
GROUP = 8
NPHM = 4
PAD = 16
CTX = ("y", "zl")
DP = ("zh", "x", "c")
SCALE = 1.0 / math.sqrt(HD)
LOG2E = 1.4426950408889634
SMEM = pl.BlockSpec(memory_space=pltpu.SMEM)
F32 = jnp.float32
BF16 = jnp.bfloat16


def dot(a, b, ca, cb):
    return lax.dot_general(a, b, (((ca,), (cb,)), ((), ())), preferred_element_type=F32)


def around(distance):
    return [(i, (i + distance) % NPHM) for i in range(NPHM)]


def params(mib):
    return pltpu.CompilerParams(vmem_limit_bytes=mib << 20)


def chunks(x, steps):
    tok, width = x.shape[1:]
    wide = width // NPHM // steps
    return [
        pl.BlockSpec((1, tok, wide), functools.partial(lambda a, j: (0, 0, a * steps + j), a))
        for a in range(NPHM)
    ]


def stacked(xs):
    return jnp.concatenate([xs[n * NPHM + a][0] for a in range(NPHM) for n in range(2)], axis=0)


def project_kernel(mix, core, *refs):
    xs, (w, part, out) = refs[:8], refs[8:]
    j = pl.program_id(0)
    tok = xs[0].shape[1]
    one = dot(stacked(xs), jnp.concatenate([w[i] for i in range(NPHM)], axis=1), 1, 0)

    @pl.when(j == 0)
    def _():
        for a in range(NPHM):
            part[a] = one[2 * a * tok : 2 * (a + 1) * tok]

    @pl.when(j > 0)
    def _():
        for a in range(NPHM):
            part[a] = part[a] + one[2 * a * tok : 2 * (a + 1) * tok]

    @pl.when(j == pl.num_programs(0) - 1)
    def _():
        for b in range(NPHM):
            total = None
            for a in range(NPHM):
                for i in range(NPHM):
                    term = mix[i * 16 + a * 4 + b] * part[a, :, i * HD : (i + 1) * HD]
                    total = term if total is None else total + term
            total = total.astype(BF16)
            out[core[0], b] = total[:tok]
            out[1 - core[0], b] = total[tok:]


def project(mix, core, xm, xo, w):
    tok, width = xm.shape[1:]
    dq, cols = width // NPHM, NPHM * HD
    steps = 4
    return pl.pallas_call(
        project_kernel,
        grid=(steps,),
        in_specs=[SMEM, SMEM]
        + chunks(xm, steps)
        + chunks(xo, steps)
        + [pl.BlockSpec((NPHM, dq // steps, HD), lambda j: (0, j, 0))],
        out_specs=[
            pl.BlockSpec((NPHM, 2 * tok, cols), lambda j: (0, 0, 0)),
            pl.BlockSpec((2, NPHM, tok, HD), lambda j: (0, 0, 0, 0)),
        ],
        out_shape=[
            jax.ShapeDtypeStruct((NPHM, 2 * tok, cols), F32),
            jax.ShapeDtypeStruct((2, NPHM, tok, HD), BF16),
        ],
        compiler_params=params(32),
    )(mix, core, *([xm] * 4), *([xo] * 4), w)


def attend_kernel(
    where, lens, q0, q1, q2, q3, row, before, back, own, *scratch
):
    q, do, keys, values, gk, gv, bias, probs, dscores = scratch
    tok = q0.shape[1]
    win = (REACH + 1) * tok
    o = pl.program_id(0)

    @pl.when(o == 0)
    def _():
        for n in range(REACH):
            keys[n * tok : (n + 1) * tok] = before[0, n]
            values[n * tok : (n + 1) * tok] = before[1, n]
        for n in range(KVH):
            at = slice((REACH + n) * tok, (REACH + n + 1) * tok)
            keys[at] = row[0, n]
            values[at] = row[1, n]
        gk[...] = jnp.zeros_like(gk)
        gv[...] = jnp.zeros_like(gv)

    for n, block in enumerate((q0, q1, q2, q3)):

        @pl.when(o == n)
        def _(block=block):
            for r in range(GROUP):
                q[r * tok : (r + 1) * tok] = block[0, :, r * HD : (r + 1) * HD]
                do[r * tok : (r + 1) * tok] = block[1, :, r * HD : (r + 1) * HD]

    run = (where[1] + KVH - o) & (KVH - 1)
    start = (where[0] * KVH + run) * tok
    qpos = start + lax.broadcasted_iota(jnp.int32, (8, tok), 1)

    def step(n, carry):
        end, first = carry
        end = end + lens[n]
        return end, jnp.where(end <= qpos, end, first)

    _, first = lax.fori_loop(
        0, lens.shape[0], step, (jnp.int32(0), jnp.zeros((8, tok), jnp.int32))
    )
    kpos = start - REACH * tok + lax.broadcasted_iota(jnp.int32, (win, tok), 0)
    ok = (kpos >= first[0:1]) & (kpos <= qpos[0:1])
    once = jnp.where(ok, 0.0, -1e30).astype(F32)
    bias[:, :tok] = once
    bias[:, tok:] = once

    here = pl.ds(pl.multiple_of(run * tok, tok), win)
    k = keys[here, :]
    v = values[here, :]
    for r in range(0, GROUP, 2):
        rows = slice(r * tok, (r + 2) * tok)
        s = dot(k, q[rows], 1, 1) * (SCALE * LOG2E) + bias[...]
        dp = dot(v, do[rows], 1, 1)
        e = jnp.exp2(s - jnp.max(s, axis=0, keepdims=True))
        p = e * (1.0 / jnp.sum(e, axis=0, keepdims=True))
        delta = jnp.sum(p * dp, axis=0, keepdims=True)
        probs[:, rows] = p.astype(BF16)
        dscores[:, rows] = (p * (dp - delta)).astype(BF16)
    gk[here, :] = gk[here, :] + dot(dscores[...], q[...], 1, 0) * SCALE
    gv[here, :] = gv[here, :] + dot(probs[...], do[...], 1, 0)

    @pl.when(o == KVH - 1)
    def _():
        for n in range(REACH):
            back[0, n] = gk[n * tok : (n + 1) * tok].astype(BF16)
            back[1, n] = gv[n * tok : (n + 1) * tok].astype(BF16)
        for n in range(KVH):
            at = slice((REACH + n) * tok, (REACH + n + 1) * tok)
            own[0, n] = gk[at]
            own[1, n] = gv[at]


def attend(where, lens, qs, row, before):
    tok = row.shape[2]
    win, span = (REACH + 1) * tok, (REACH + KVH) * tok
    wide = GROUP * HD

    def whole(*shape):
        return pl.BlockSpec(shape, lambda o: (0,) * len(shape))

    return pl.pallas_call(
        attend_kernel,
        grid=(KVH,),
        in_specs=[SMEM, SMEM]
        + [whole(2, tok, wide)] * KVH
        + [whole(2, KVH, tok, HD), whole(2, REACH, tok, HD)],
        out_specs=[whole(2, REACH, tok, HD), whole(2, KVH, tok, HD)],
        out_shape=[
            jax.ShapeDtypeStruct((2, REACH, tok, HD), BF16),
            jax.ShapeDtypeStruct((2, KVH, tok, HD), F32),
        ],
        scratch_shapes=[
            pltpu.VMEM((GROUP * tok, HD), BF16),
            pltpu.VMEM((GROUP * tok, HD), BF16),
            pltpu.VMEM((span, HD), BF16),
            pltpu.VMEM((span, HD), BF16),
            pltpu.VMEM((span, HD), F32),
            pltpu.VMEM((span, HD), F32),
            pltpu.VMEM((win, 2 * tok), F32),
            pltpu.VMEM((win, GROUP * tok), BF16),
            pltpu.VMEM((win, GROUP * tok), BF16),
        ],
        compiler_params=params(24),
    )(where, lens, *qs, row, before)


def mixing_line(part, grads):
    sums = []
    for i in range(NPHM):
        for a in range(NPHM):
            for b in range(NPHM):
                both = part[a, :, i * HD : (i + 1) * HD] * grads[:, b * HD : (b + 1) * HD]
                sums.append(jnp.sum(both, axis=0, keepdims=True))
    sums = jnp.sum(jnp.concatenate(sums, axis=0), axis=1, keepdims=True)
    many = NPHM**3
    spot = lax.broadcasted_iota(jnp.int32, (many, HD), 0)
    lane = lax.broadcasted_iota(jnp.int32, (many, HD), 1)
    return jnp.sum(jnp.where(spot == lane, sums, 0.0), axis=0, keepdims=True)


def factor_kernel(which, mix, core, *refs):
    xs, g, refs = refs[:8], refs[8], refs[9:]
    (mixed, grads), refs = refs[-2:], refs[:-2]
    tok = g.shape[2]

    @pl.when(pl.program_id(0) == 0)
    def _():
        for b in range(NPHM):
            grads[:tok, b * HD : (b + 1) * HD] = g[core[0], b].astype(F32)
            grads[tok:, b * HD : (b + 1) * HD] = g[1 - core[0], b].astype(F32)
        for a in range(NPHM):
            for n, i in enumerate(which):
                total = mix[i * 16 + a * 4] * grads[:, :HD]
                for b in range(1, NPHM):
                    total = total + mix[i * 16 + a * 4 + b] * grads[:, b * HD : (b + 1) * HD]
                mixed[n * HD : (n + 1) * HD, 2 * a * tok : 2 * (a + 1) * tok] = total.T.astype(BF16)
        if 0 in which:
            line = mixing_line(refs[0], grads)
            line = line + jnp.concatenate([line[:, HD // 2 :], line[:, : HD // 2]], axis=1)
            line = jnp.broadcast_to(split_line(line), (PAD, HD)).astype(BF16)
            for d in range(refs[-1].shape[0]):
                refs[-1][d] = line

    total = dot(mixed[...], stacked(xs), 1, 0)
    outs = refs[1:3] if 0 in which else refs[:2]
    for n, out in enumerate(outs):
        out[...] = total[n * HD : (n + 1) * HD].astype(BF16)


def factor_grads(which, mix, core, xm, xo, g, part=None, n=0):
    tok, width = xm.shape[1:]
    dq, cols = width // NPHM, NPHM * HD
    steps = 4
    ins = [SMEM, SMEM] + chunks(xm, steps) + chunks(xo, steps)
    ins.append(pl.BlockSpec((2, NPHM, tok, HD), lambda j: (0, 0, 0, 0)))
    args = [mix, core] + [xm] * 4 + [xo] * 4 + [g]
    out_specs = [pl.BlockSpec((HD, dq // steps), lambda j: (0, j))] * 2
    out_shape = [jax.ShapeDtypeStruct((HD, dq), BF16)] * 2
    if part is not None:
        ins.append(pl.BlockSpec((NPHM, 2 * tok, cols), lambda j: (0, 0, 0)))
        args.append(part)
        out_specs.append(pl.BlockSpec((n, PAD, HD), lambda j: (0, 0, 0)))
        out_shape.append(jax.ShapeDtypeStruct((n, PAD, HD), BF16))
    return pl.pallas_call(
        functools.partial(factor_kernel, which),
        grid=(steps,),
        in_specs=ins,
        out_specs=out_specs,
        out_shape=out_shape,
        scratch_shapes=[
            pltpu.VMEM((2 * HD, NPHM * 2 * tok), BF16),
            pltpu.VMEM((2 * tok, cols), F32),
        ],
        compiler_params=params(32),
    )(*args)


def split_line(value):
    lane = lax.broadcasted_iota(jnp.int32, value.shape, 1)
    high = value.astype(BF16).astype(F32)
    return jnp.where(lane < HD // 2, high, value - high)


def turn_kernel(t0, t1, t2, t3, out):
    n, rows = out.shape[:2]
    total = t0[...].astype(F32)
    for t in (t1, t2, t3):
        total = total + t[...].astype(F32)
    turned = total.T.astype(BF16)
    for d in range(n):
        out[d] = turned[d * rows : (d + 1) * rows]


def turn(terms, n):
    rows = terms[0].shape[1] // n
    return pl.pallas_call(
        turn_kernel,
        out_shape=jax.ShapeDtypeStruct((n, rows, HD), BF16),
        compiler_params=params(40),
    )(*terms)


def total_kernel(blocks, lines, out):
    rows = blocks.shape[1]
    total, line = blocks[0].astype(F32), lines[0].astype(F32)
    for d in range(1, blocks.shape[0]):
        total = total + blocks[d].astype(F32)
        line = line + lines[d].astype(F32)
    line = line + jnp.concatenate([line[:, HD // 2 :], line[:, : HD // 2]], axis=1)
    line = split_line(line).astype(BF16)
    body = total.astype(BF16)
    for d in range(out.shape[0]):
        out[d, :rows] = body
        out[d, rows:] = line


def total(blocks, lines, n):
    rows = blocks.shape[1] + PAD
    return pl.pallas_call(
        total_kernel,
        out_shape=jax.ShapeDtypeStruct((n, rows, HD), BF16),
        compiler_params=params(40),
    )(blocks, lines)


def final_kernel(blocks, gk, gv, mk, mv):
    half = NPHM * 2
    rows = gk.shape[0]
    lines = [None, None]
    for i in range(NPHM):
        for c, out in enumerate((gk, gv)):
            at = i * 2 + c
            block = blocks[at].astype(F32)
            for z in range(at + half, blocks.shape[0], half):
                block = block + blocks[z].astype(F32)
            out[:, i, :] = block[:rows]
            line = block[rows : rows + 1]
            lines[c] = line if lines[c] is None else lines[c] + line
    row = lax.broadcasted_iota(jnp.int32, (NPHM, HD), 0)
    lane = lax.broadcasted_iota(jnp.int32, (NPHM, HD), 1)
    col = lax.broadcasted_iota(jnp.int32, (NPHM, NPHM), 1)
    for line, out in zip(lines, (mk, mv)):
        for i in range(NPHM):
            tile = jnp.zeros((NPHM, NPHM), F32)
            for b in range(NPHM):
                mine = (lane & (HD // 2 - 1)) == i * 16 + row * 4 + b
                tile = jnp.where(col == b, jnp.sum(jnp.where(mine, line, 0.0), axis=1, keepdims=True), tile)
            out[i] = tile


def final(blocks, rows):
    return pl.pallas_call(
        final_kernel,
        out_shape=[jax.ShapeDtypeStruct((rows, NPHM, HD), F32)] * 2
        + [jax.ShapeDtypeStruct((NPHM, NPHM, NPHM), F32)] * 2,
        compiler_params=params(40),
    )(blocks)


def shards(inputs, queries, upstream, lengths, factor_k, factor_v, mixing_k, mixing_v):
    tok = inputs.shape[1]
    rows = factor_k.shape[0]
    n_ctx = lax.axis_size("y") * lax.axis_size("zl")
    n_dp = lax.axis_size("zh") * lax.axis_size("x") * lax.axis_size("c")
    z_at = lax.axis_index("zl")
    x_at = lax.axis_index("x")
    first = lax.axis_index("c") == 0
    swap = [(0, 1), (1, 0)]

    other = lax.ppermute(inputs, "c", swap)
    mix = jnp.where(first, mixing_k, mixing_v)
    turned = lax.dynamic_slice_in_dim(jnp.concatenate([mix, mix]), x_at, NPHM, 0).reshape(-1)
    mine = lax.dynamic_index_in_dim(
        jnp.where(first, factor_k, factor_v), x_at, axis=1, keepdims=False
    )
    n_y, n_z = lax.axis_size("y"), lax.axis_size("zl")
    core = lax.axis_index("c").astype(jnp.int32).reshape(1)
    piece = jnp.broadcast_to(mine[None], (n_z, rows, HD))
    wide = GROUP * HD
    blocks = []
    for o in range(KVH):
        head = ((z_at + o) & (KVH - 1)) * wide
        blocks.append(
            jnp.stack([lax.dynamic_slice_in_dim(m[0], head, wide, 1) for m in (queries, upstream)])
        )
    piece = lax.all_to_all(piece, "zl", 0, 0, tiled=True).reshape(1, n_z * rows, HD)
    piece = lax.all_to_all(
        jnp.broadcast_to(piece, (n_y, n_z * rows, HD)), "y", 0, 0, tiled=True
    ).reshape(1, n_ctx * rows, HD)
    q1 = lax.ppermute(blocks[1], "zl", around(1))
    piece, q1, b2 = lax.optimization_barrier((piece, q1, blocks[2]))
    q2 = lax.ppermute(b2, "zl", around(2))
    weights = lax.all_to_all(
        jnp.broadcast_to(piece, (NPHM, n_ctx * rows, HD)), "x", 0, 0, tiled=True
    )
    weights, q2, b3 = lax.optimization_barrier((weights, q2, blocks[3]))
    q3 = lax.ppermute(b3, "zl", around(3))
    part, both = project(mix.reshape(-1), core, inputs, other, weights)

    both, q3 = lax.optimization_barrier((both, q3))
    row = lax.all_to_all(both.reshape(2 * KVH, tok, HD), ("c", "zl"), 0, 0, tiled=True)
    row = row.reshape(2, KVH, tok, HD)
    up = [(n, n + 1) for n in range(lax.axis_size("y") - 1)]
    before = lax.ppermute(row[:, KVH - REACH :], "y", up)
    where = jnp.stack([lax.axis_index("y"), z_at]).astype(jnp.int32)
    back, own = attend(where, lengths[0], [blocks[0], q1, q2, q3], row, before)
    back = lax.ppermute(back, "y", [(n, m) for m, n in up]).astype(F32)
    own = own + jnp.pad(back, ((0, 0), (KVH - REACH, 0), (0, 0), (0, 0)))
    grads = own.astype(BF16).reshape(2 * KVH, tok, HD)
    grads = lax.all_to_all(grads, ("c", "zl"), 0, 0, tiled=True).reshape(2, KVH, tok, HD)

    one, three = factor_grads((1, 3), turned, core, inputs, other, grads)
    sent = [lax.ppermute(one, "x", around(1)), lax.ppermute(three, "x", around(3))]
    own, two, lines = factor_grads((0, 2), turned, core, inputs, other, grads, part, n_ctx)
    sent.append(lax.ppermute(two, "x", around(2)))
    lines = lax.all_to_all(lines, CTX, 0, 0, tiled=True)
    blocks = lax.all_to_all(turn([own] + sent, n_ctx), CTX, 0, 0, tiled=True)
    blocks = lax.all_to_all(total(blocks, lines, n_dp), DP, 0, 0, tiled=True)
    return tuple(final(blocks, rows))


def solution(mesh):
    n_dp, n_ctx = mesh.devices.shape
    zl = 4
    shape = (n_dp // 8, 4, 2, n_ctx // zl, zl)
    wide = Mesh(mesh.devices.reshape(shape), DP + CTX)
    in_specs = (
        P(DP, CTX, None),
        P(DP, CTX, None),
        P(DP, CTX, None),
        P(DP, None),
        P(CTX, None, None),
        P(CTX, None, None),
        P(),
        P(),
    )
    out_specs = (P(CTX, None, None), P(CTX, None, None), P(), P())
    return jax.shard_map(shards, mesh=wide, in_specs=in_specs, out_specs=out_specs, check_vma=False)
```

time: 236 us -> 230 us (0.975)
  blocking collectives: 63.7 us -> 55.9 us
  waiting for transfers between devices: 66 us -> 71.8 us
    all_to_all x2 -> x4, waiting for transfers between devices: 5.69 us -> 23.4 us  [the longest x1 9.06 us: shards(): lax.all_to_all(both.reshape(2 * KVH, tok, HD), ('c', 'zl'), 0, 0, tiled=T...]
    ppermute x1, waiting for transfers between devices: 16.9 us -> 6.75 us  [shards(): q1 = lax.ppermute(blocks[1], 'zl', around(1))]
    ppermute x3 -> x1, starting transfers between devices: 12.9 us -> 3.08 us  [shards(): before = lax.ppermute(row[:, KVH - REACH:], 'y', up)]
    all_to_all x2 -> x4, starting transfers between devices: 16.9 us -> 25.1 us  [the longest x1 8.3 us: shards(): lines = lax.all_to_all(lines, CTX, 0, 0, tiled=True)]
    all_to_all x3, blocking collectives: 63.7 us -> 55.9 us  [the longest x1 26.1 us: shards(): blocks = lax.all_to_all(total(blocks, lines, n_dp), DP, 0, 0, tiled=True)]
    ppermute x1, waiting for transfers between devices: 11.6 us -> 4.13 us  [shards(): lax.ppermute(one, 'x', around(1))]
    ppermute x1, waiting for transfers between devices: 0.01 us -> 4.89 us  [shards(): q3 = lax.ppermute(b3, 'zl', around(3))]
    unnamed x16 -> x14, local copies, waits for them, and re-layouts: 4.78 us -> 3.61 us
  transfers between devices with their start and end apart: 14 -> 14, of which waited for: 9 -> 9; matrix products, arithmetic and copies ran while one was open for 4% -> 4% of each run, Pallas kernels for 4% -> 5%
where the time goes in v3:
time: 230 us; the launch traced here: 228 us
  waiting for transfers between devices  71.8 us (31%)
  starting transfers between devices  56.2 us (24%)
  blocking collectives  55.9 us (24%)
  Pallas kernels  28.6 us (12%)
  local copies, waits for them, and re-layouts  10 us (4%)
  other arithmetic  4.65 us (2%)
    all_to_all x1, blocking collectives, shards(): blocks = lax.all_to_all(total(blocks, lines, n_dp), DP, 0, 0, tiled=True)  26.1 us
    ppermute x1, waiting for transfers between devices, shards(): q2 = lax.ppermute(b2, 'zl', around(2))  23 us
    all_to_all x1, blocking collectives, shards(): blocks = lax.all_to_all(turn([own] + sent, n_ctx), CTX, 0, 0, tiled=True)  17.6 us
    all_to_all x1, blocking collectives, shards(): lax.all_to_all(piece, 'zl', 0, 0, tiled=True).reshape(1, n_z * rows, HD)  12.2 us
    pallas_call x2, Pallas kernels, factor_grads(): pl.pallas_call(functools.partial(factor_kernel, which), grid=(steps,), in...  11 us
    pallas_call x1, Pallas kernels, attend(): pl.pallas_call(attend_kernel, grid=(KVH,), in_specs=[SMEM, SMEM] + [whole...  10.2 us
    all_to_all x1, waiting for transfers between devices, shards(): lax.all_to_all(both.reshape(2 * KVH, tok, HD), ('c', 'zl'), 0, 0, tiled=T...  9.06 us
    all_to_all x1, waiting for transfers between devices, shards(): lax.all_to_all(grads, ('c', 'zl'), 0, 0, tiled=True)  8.94 us
  transfers between devices with their start and end apart: 14, of which 9 were waited for; matrix products, arithmetic and copies ran while one was open for 4% of the time, Pallas kernels for 5%

profile of v3, /device:TPU:1, one launch (start us, length us, event | category | flops | bytes accessed | tf_op | source)
XLA Modules:
  0.0 228.0 jit_solution(5711052544136530058)
XLA Ops:
  0.6 1.0 constant_dynamic-slice_fusion.6
  1.6 12.2 %all_to_all.40 = bf16[4,64,128]{2,1,0:T(8,128)(2,1)S(1)} all-to-all(bf16[4,64,128]{2,1,0:T(8,128)(2,1)S(1)} %broadcast_in_dim.23), channel_id=1, replica_groups=mesh['zh'=2,'x'=4,'c'=2,'y'=8,'zl'=4] {'zl'}, dimensions={0} | all-to-all | bytes 131072 | tf_op jit(solution)/shard_map/all_to_all | solution.py:388
  13.8 0.9 broadcast_in_dim.25
  14.7 6.8 %all-to-all-start.1 = ((bf16[8,256,128]{2,1,0:T(8,128)(2,1)}), bf16[8,256,128]{2,1,0:T(8,128)(2,1)S(1)}, u32[]{:S(2)}, u32[]{:S(2)}) async-start(bf16[8,256,128]{2,1,0:T(8,128)(2,1)} %broadcast_in_dim.25), calls=%async_computation.1 | async-start | bytes 1048576 | tf_op jit(solution)/shard_map/all_to_all | solution.py:389
  21.5 0.0 copy-start
  21.5 2.7 %constant_dynamic-slice_fusion = (bf16[1,128,1024]{2,1,0:T(8,128)(2,1)S(1)}, bf16[1,128,1024]{2,1,0:T(8,128)(2,1)S(1)}, bf16[1,128,1024]{2,1,0:T(8,128)(2,1)}, b...) fusion(bf16[1,128,4096]{2,1,0:T(8,128)(2,1)} %param.10, ...), kind=kLoop, calls=%fused_computation.11 | loop fusion | bytes 4194320 | tf_op jit(solution)/shard_map/dynamic_slice | solution.py:386
  24.2 0.1 pad_maximum_fusion.1
  24.3 2.5 %collective-permute-start.1 = (bf16[2,128,1024]{2,1,0:T(8,128)(2,1)S(1)}, bf16[2,128,1024]{2,1,0:T(8,128)(2,1)S(1)}, u32[]{:S(2)}, u32[]{:S(2)}) collective-permute-start(bf16[2,128,1024]{2,1,0:T(8,128)(2,1)S(1)} %pad_maximum_fusion.1), channel_id=1, source_target_pairs={{0,1},{1,2},{2,3},{3,0},{4,5},{5,6},{6,7},{7,4},{8,9},{9,10},{10,1... | collective-permute-start | bytes 1572872 | tf_op jit(solution)/shard_map/ppermute | solution.py:392
  26.9 0.0 copy-done
  26.9 4.6 %collective-permute-start = (bf16[1,128,8192]{2,1,0:T(8,128)(2,1)S(1)}, bf16[1,128,8192]{2,1,0:T(8,128)(2,1)}, u32[]{:S(2)}, u32[]{:S(2)}) collective-permute-start(bf16[1,128,8192]{2,1,0:T(8,128)(2,1)S(1)} %copy-done), channel_id=1, source_target_pairs={{0,32},{32,0},{1,33},{33,1},{2,34},{34,2},{3,35},{35,3},{4,36},{36... | collective-permute-start | bytes 6291464 | tf_op jit(solution)/shard_map/ppermute | solution.py:372
  31.4 0.8 pad_maximum_fusion.2
  32.3 6.7 %collective-permute-done.1.q1 = bf16[2,128,1024]{2,1,0:T(8,128)(2,1)S(1)} collective-permute-done((bf16[2,128,1024]{2,1,0:T(8,128)(2,1)S(1)}, bf16[2,128,1024]{2,1,0:T(8,128)(2,1)S(1)}, u32[]{:S(2)}, u32[]{:S(2)}) %collective-permute-start.1) | collective-permute-done | bytes 524320 | tf_op jit(solution)/shard_map/ppermute | solution.py:392
  39.0 0.0 all-to-all-done.1
  39.0 1.6 broadcast_in_dim.27
  40.7 0.0 copy-start.5
  40.7 0.0 copy-start.6
  40.7 4.6 %all-to-all-start.2 = ((bf16[4,2048,128]{2,1,0:T(8,128)(2,1)}), bf16[4,2048,128]{2,1,0:T(8,128)(2,1)}, u32[]{:S(2)}, u32[]{:S(2)}) async-start(bf16[4,2048,128]{2,1,0:T(8,128)(2,1)} %broadcast_in_dim.27), calls=%async_computation.2 | async-start | bytes 4194304 | tf_op jit(solution)/shard_map/all_to_all | solution.py:395
  45.3 1.9 collective-permute-start.2
  47.2 1.8 pad_maximum_fusion.3
  49.0 23.0 %collective-permute-done.2.q2 = bf16[2,128,1024]{2,1,0:T(8,128)(2,1)S(1)} collective-permute-done((bf16[2,128,1024]{2,1,0:T(8,128)(2,1)}, bf16[2,128,1024]{2,1,0:T(8,128)(2,1)S(1)}, u32[]{:S(2)}, u32[]{:S(2)}) %collective-permute-start.2) | collective-permute-done | bytes 524320 | tf_op jit(solution)/shard_map/ppermute | solution.py:394
  72.0 0.0 all-to-all-done.2.refs_8_
  72.0 1.9 collective-permute-start.3
  73.9 0.0 copy-done.5
  74.0 0.0 copy-done.6
  74.0 0.1 reshape.55.mix
  74.1 0.0 collective-permute-done.refs_4_.refs_5_.refs_6_.refs_7_
  74.1 0.0 copy-start.4
  74.1 6.1 %shard_map.111 = (f32[4,256,512]{2,1,0:T(8,128)S(1)}, bf16[2,4,128,128]{3,2,1,0:T(8,128)(2,1)S(1)}) custom-call(f32[64]{0:T(128)S(1)} %reshape.55.mix, s32[1]{0:T(128)} %bitcast.core, bf16[1,128,8192]{2,1,0:T(8,128)(2,1)S(1)} %copy-done, bf16[1,128,8192]{2,1,0:T(8,128)(2,1)S(1)} %copy-done, bf16[1,128,8192]{2,1,0:T(8,128)(2,1)S(1)} %copy-done, ...), custom_call_target="tpu_custom_call" | custom-call | tf_op jit(solution)/shard_map/pallas_call | solution.py:84
  80.2 0.0 copy-start.1
  80.2 1.3 copy-done.1
  81.5 0.0 copy-start.3
  81.5 0.7 copy-done.3
  82.2 4.9 %collective-permute-done.3.q3 = bf16[2,128,1024]{2,1,0:T(8,128)(2,1)} collective-permute-done((bf16[2,128,1024]{2,1,0:T(8,128)(2,1)}, bf16[2,128,1024]{2,1,0:T(8,128)(2,1)}, u32[]{:S(2)}, u32[]{:S(2)}) %collective-permute-start.3) | collective-permute-done | bytes 524320 | tf_op jit(solution)/shard_map/ppermute | solution.py:399
  87.1 4.8 %all-to-all-start.3 = ((bf16[8,128,128]{2,1,0:T(8,128)(2,1)}), bf16[8,128,128]{2,1,0:T(8,128)(2,1)S(1)}, u32[]{:S(2)}, u32[]{:S(2)}) async-start(bf16[8,128,128]{2,1,0:T(8,128)(2,1)} %bitcast.20), calls=%async_computation.3 | async-start | bytes 524288 | tf_op jit(solution)/shard_map/all_to_all | solution.py:403
  91.9 9.1 %all-to-all-done.3 = bf16[8,128,128]{2,1,0:T(8,128)(2,1)S(1)} async-done(((bf16[8,128,128]{2,1,0:T(8,128)(2,1)}), bf16[8,128,128]{2,1,0:T(8,128)(2,1)S(1)}, u32[]{:S(2)}, u32[]{:S(2)}) %all-to-all-start.3) | async-done | bytes 262176 | tf_op jit(solution)/shard_map/all_to_all | solution.py:403
  101.0 3.1 %collective-permute-start.4 = (bf16[2,3,128,128]{3,2,1,0:T(8,128)(2,1)S(1)}, bf16[2,3,128,128]{3,2,1,0:T(8,128)(2,1)S(1)}, u32[]{:S(2)}, u32[]{:S(2)}) collective-permute-start(bf16[2,3,128,128]{3,2,1,0:T(8,128)(2,1)S(1)} %slice.4), channel_id=1, source_target_pairs={{0,4},{4,8},{8,12},{12,16},{16,20},{20,24},{24,28},{1,5},{5,9},{9,... | collective-permute-start | bytes 589832 | tf_op jit(solution)/shard_map/ppermute | solution.py:406
  104.1 0.1 pad_add_fusion.where
  104.2 1.1 pad_maximum_fusion.q0
  105.3 2.8 %collective-permute-done.4.before = bf16[2,3,128,128]{3,2,1,0:T(8,128)(2,1)S(1)} collective-permute-done((bf16[2,3,128,128]{3,2,1,0:T(8,128)(2,1)S(1)}, bf16[2,3,128,128]{3,2,1,0:T(8,128)(2,1)S(1)}, u32[]{:S(2)}, u32[]{:S(2)}) %collective-permute-start.4) | collective-permute-done | bytes 196640 | tf_op jit(solution)/shard_map/ppermute | solution.py:406
  108.0 0.0 copy-done.4
  108.0 10.2 %shard_map.112 = (bf16[2,3,128,128]{3,2,1,0:T(8,128)(2,1)S(1)}, f32[2,4,128,128]{3,2,1,0:T(8,128)S(1)}) custom-call(s32[2]{0:T(128)S(1)} %pad_add_fusion.where, s32[32]{0:T(128)S(1)} %bitcast.21, bf16[2,128,1024]{2,1,0:T(8,128)(2,1)S(1)} %pad_maximum_fusion.q0, bf16[2,128,1024]{2,1,0:T(8,128)(2,1)S(1)} %collective-permute-done.1.q1, ...), custom_call_target="tpu_custom_call" | custom-call | tf_op jit(solution)/shard_map/pallas_call | solution.py:183
  118.2 1.3 collective-permute-start.5
  119.5 6.9 %collective-permute-done.5 = bf16[2,3,128,128]{3,2,1,0:T(8,128)(2,1)S(1)} collective-permute-done((bf16[2,3,128,128]{3,2,1,0:T(8,128)(2,1)S(1)}, bf16[2,3,128,128]{3,2,1,0:T(8,128)(2,1)S(1)}, u32[]{:S(2)}, u32[]{:S(2)}) %collective-permute-start.5) | collective-permute-done | bytes 196640 | tf_op jit(solution)/shard_map/ppermute | solution.py:409
  126.4 0.8 add_convert_fusion
  127.1 5.1 %all-to-all-start.4 = ((bf16[8,128,128]{2,1,0:T(8,128)(2,1)}), bf16[8,128,128]{2,1,0:T(8,128)(2,1)S(1)}, u32[]{:S(2)}, u32[]{:S(2)}) async-start(bf16[8,128,128]{2,1,0:T(8,128)(2,1)} %bitcast.10), calls=%async_computation.4 | async-start | bytes 524288 | tf_op jit(solution)/shard_map/all_to_all | solution.py:412
  132.3 0.1 reshape.52.mix
  132.4 8.9 %all-to-all-done.4 = bf16[8,128,128]{2,1,0:T(8,128)(2,1)S(1)} async-done(((bf16[8,128,128]{2,1,0:T(8,128)(2,1)}), bf16[8,128,128]{2,1,0:T(8,128)(2,1)S(1)}, u32[]{:S(2)}, u32[]{:S(2)}) %all-to-all-start.4) | async-done | bytes 262176 | tf_op jit(solution)/shard_map/all_to_all | solution.py:412
  141.3 0.0 copy-start.2
  141.3 1.6 copy-done.2
  142.9 6.0 %shard_map.113 = (bf16[128,2048]{1,0:T(8,128)(2,1)S(1)}, bf16[128,2048]{1,0:T(8,128)(2,1)}, bf16[32,16,128]{2,1,0:T(8,128)(2,1)}) custom-call(f32[64]{0:T(128)S(1)} %reshape.52.mix, s32[1]{0:T(128)} %bitcast.core, bf16[1,128,8192]{2,1,0:T(8,128)(2,1)S(1)} %copy-done, bf16[1,128,8192]{2,1,0:T(8,128)(2,1)S(1)} %copy-done, bf16[1,128,8192]{2,1,0:T(8,128)(2,1)S(1)} %copy-done, ...), custom_call_target="tpu_custom_call" | custom-call | tf_op jit(solution)/shard_map/pallas_call | solution.py:266
  148.8 4.7 %collective-permute-start.8 = (bf16[128,2048]{1,0:T(8,128)(2,1)}, bf16[128,2048]{1,0:T(8,128)(2,1)S(1)}, u32[]{:S(2)}, u32[]{:S(2)}) collective-permute-start(bf16[128,2048]{1,0:T(8,128)(2,1)} %get-tuple-element.36), channel_id=1, source_target_pairs={{0,128},{64,192},{128,0},{192,64},{1,129},{65,193},{129,1},{193,65... | collective-permute-start | bytes 1572872 | tf_op jit(solution)/shard_map/ppermute | solution.py:417
  153.6 5.0 %shard_map.114 = (bf16[128,2048]{1,0:T(8,128)(2,1)}, bf16[128,2048]{1,0:T(8,128)(2,1)}) custom-call(f32[64]{0:T(128)S(1)} %reshape.52.mix, s32[1]{0:T(128)} %bitcast.core, bf16[1,128,8192]{2,1,0:T(8,128)(2,1)S(1)} %copy-done, bf16[1,128,8192]{2,1,0:T(8,128)(2,1)S(1)} %copy-done, bf16[1,128,8192]{2,1,0:T(8,128)(2,1)S(1)} %copy-done, ...), custom_call_target="tpu_custom_call" | custom-call | tf_op jit(solution)/shard_map/pallas_call | solution.py:266
  158.6 2.2 collective-permute-start.6
  160.8 4.3 %collective-permute-start.7 = (bf16[128,2048]{1,0:T(8,128)(2,1)}, bf16[128,2048]{1,0:T(8,128)(2,1)S(1)}, u32[]{:S(2)}, u32[]{:S(2)}) collective-permute-start(bf16[128,2048]{1,0:T(8,128)(2,1)} %get-tuple-element.35), channel_id=1, source_target_pairs={{0,192},{64,0},{128,64},{192,128},{1,193},{65,1},{129,65},{193,129... | collective-permute-start | bytes 1572872 | tf_op jit(solution)/shard_map/ppermute | solution.py:415
  165.1 8.3 %all-to-all-start.6 = ((bf16[32,16,128]{2,1,0:T(8,128)(2,1)}), bf16[32,16,128]{2,1,0:T(8,128)(2,1)S(1)}, u32[]{:S(2)}, u32[]{:S(2)}) async-start(bf16[32,16,128]{2,1,0:T(8,128)(2,1)} %get-tuple-element.37), calls=%async_computation.6 | async-start | bytes 262144 | tf_op jit(solution)/shard_map/all_to_all | solution.py:418
  173.4 0.0 collective-permute-done.8.t3
  173.4 4.1 %collective-permute-done.6.t1 = bf16[128,2048]{1,0:T(8,128)(2,1)S(1)} collective-permute-done((bf16[128,2048]{1,0:T(8,128)(2,1)}, bf16[128,2048]{1,0:T(8,128)(2,1)S(1)}, u32[]{:S(2)}, u32[]{:S(2)}) %collective-permute-start.6) | collective-permute-done | bytes 524320 | tf_op jit(solution)/shard_map/ppermute | solution.py:415
  177.5 0.0 collective-permute-done.7.t2
  177.5 0.4 shard_map.115
  177.9 5.4 %all-to-all-done.6.lines = bf16[32,16,128]{2,1,0:T(8,128)(2,1)S(1)} async-done(((bf16[32,16,128]{2,1,0:T(8,128)(2,1)}), bf16[32,16,128]{2,1,0:T(8,128)(2,1)S(1)}, u32[]{:S(2)}, u32[]{:S(2)}) %all-to-all-start.6) | async-done | bytes 131104 | tf_op jit(solution)/shard_map/all_to_all | solution.py:418
  183.3 17.6 %all_to_all.41.blocks = bf16[32,64,128]{2,1,0:T(8,128)(2,1)S(1)} all-to-all(bf16[32,64,128]{2,1,0:T(8,128)(2,1)S(1)} %shard_map.115), channel_id=1, replica_groups=mesh['zh'=2,'x'=4,'c'=2,'y'=8,'zl'=4] {'y','zl'}, dimensions={0} | all-to-all | bytes 1048576 | tf_op jit(solution)/shard_map/all_to_all | solution.py:419
  200.9 0.1 shard_map.116
  201.0 26.1 %all_to_all.42.blocks = bf16[16,80,128]{2,1,0:T(8,128)(2,1)S(1)} all-to-all(bf16[16,80,128]{2,1,0:T(8,128)(2,1)S(1)} %shard_map.116), channel_id=1, replica_groups=mesh['zh'=2,'x'=4,'c'=2,'y'=8,'zl'=4] {'zh','x','c'}, dimensions={0} | all-to-all | bytes 655360 | tf_op jit(solution)/shard_map/all_to_all | solution.py:420
  227.1 0.8 shard_map.117
  (5 shorter events, 0.1 us)
Async XLA Ops:
  14.7 24.3 %all-to-all-start.1 = ((bf16[8,256,128]{2,1,0:T(8,128)(2,1)}), bf16[8,256,128]{2,1,0:T(8,128)(2,1)S(1)}, u32[]{:S(2)}, u32[]{:S(2)}) async-start(bf16[8,256,128]{2,1,0:T(8,128)(2,1)} %broadcast_in_dim.25), calls=%async_computation.1 | async-start | bytes 1048576 | tf_op jit(solution)/shard_map/all_to_all | solution.py:389
  21.5 5.3 %copy-start = (bf16[1,128,8192]{2,1,0:T(8,128)(2,1)S(1)}, bf16[1,128,8192]{2,1,0:T(8,128)(2,1)}, u32[]{:S(2)}) copy-start(bf16[1,128,8192]{2,1,0:T(8,128)(2,1)} %refs_3_.5) | copy-start | bytes 6291460
  24.3 14.7 %collective-permute-start.1 = (bf16[2,128,1024]{2,1,0:T(8,128)(2,1)S(1)}, bf16[2,128,1024]{2,1,0:T(8,128)(2,1)S(1)}, u32[]{:S(2)}, u32[]{:S(2)}) collective-permute-start(bf16[2,128,1024]{2,1,0:T(8,128)(2,1)S(1)} %pad_maximum_fusion.1), channel_id=1, source_target_pairs={{0,1},{1,2},{2,3},{3,0},{4,5},{5,6},{6,7},{7,4},{8,9},{9,10},{10,1... | collective-permute-start | bytes 1572872 | tf_op jit(solution)/shard_map/ppermute | solution.py:392
  26.9 47.2 %collective-permute-start = (bf16[1,128,8192]{2,1,0:T(8,128)(2,1)S(1)}, bf16[1,128,8192]{2,1,0:T(8,128)(2,1)}, u32[]{:S(2)}, u32[]{:S(2)}) collective-permute-start(bf16[1,128,8192]{2,1,0:T(8,128)(2,1)S(1)} %copy-done), channel_id=1, source_target_pairs={{0,32},{32,0},{1,33},{33,1},{2,34},{34,2},{3,35},{35,3},{4,36},{36... | collective-permute-start | bytes 6291464 | tf_op jit(solution)/shard_map/ppermute | solution.py:372
  40.7 33.3 %copy-start.5 = (f32[4,4,4]{2,1,0:T(4,128)S(1)}, f32[4,4,4]{2,1,0:T(4,128)}, u32[]{:S(2)}) copy-start(f32[4,4,4]{2,1,0:T(4,128)} %param.14) | copy-start | bytes 772
  40.7 33.3 %copy-start.6 = (f32[4,4,4]{2,1,0:T(4,128)S(1)}, f32[4,4,4]{2,1,0:T(4,128)}, u32[]{:S(2)}) copy-start(f32[4,4,4]{2,1,0:T(4,128)} %param.15) | copy-start | bytes 772
  40.7 31.3 %all-to-all-start.2 = ((bf16[4,2048,128]{2,1,0:T(8,128)(2,1)}), bf16[4,2048,128]{2,1,0:T(8,128)(2,1)}, u32[]{:S(2)}, u32[]{:S(2)}) async-start(bf16[4,2048,128]{2,1,0:T(8,128)(2,1)} %broadcast_in_dim.27), calls=%async_computation.2 | async-start | bytes 4194304 | tf_op jit(solution)/shard_map/all_to_all | solution.py:395
  45.3 26.7 %collective-permute-start.2 = (bf16[2,128,1024]{2,1,0:T(8,128)(2,1)}, bf16[2,128,1024]{2,1,0:T(8,128)(2,1)S(1)}, u32[]{:S(2)}, u32[]{:S(2)}) collective-permute-start(bf16[2,128,1024]{2,1,0:T(8,128)(2,1)} %pad_maximum_fusion.2), channel_id=1, source_target_pairs={{0,2},{1,3},{2,0},{3,1},{4,6},{5,7},{6,4},{7,5},{8,10},{9,11},{10,... | collective-permute-start | bytes 1572872 | tf_op jit(solution)/shard_map/ppermute | solution.py:394
  72.0 15.1 %collective-permute-start.3 = (bf16[2,128,1024]{2,1,0:T(8,128)(2,1)}, bf16[2,128,1024]{2,1,0:T(8,128)(2,1)}, u32[]{:S(2)}, u32[]{:S(2)}) collective-permute-start(bf16[2,128,1024]{2,1,0:T(8,128)(2,1)} %pad_maximum_fusion.3), channel_id=1, source_target_pairs={{0,3},{1,0},{2,1},{3,2},{4,7},{5,4},{6,5},{7,6},{8,11},{9,8},{10,9... | collective-permute-start | bytes 1572872 | tf_op jit(solution)/shard_map/ppermute | solution.py:399
  74.1 33.9 %copy-start.4 = (s32[1,32]{1,0:T(1,128)S(1)}, s32[1,32]{1,0:T(1,128)}, u32[]{:S(2)}) copy-start(s32[1,32]{1,0:T(1,128)} %param.11) | copy-start | bytes 388
  80.2 1.3 copy-start.1
  81.5 0.7 copy-start.3
  87.1 13.9 %all-to-all-start.3 = ((bf16[8,128,128]{2,1,0:T(8,128)(2,1)}), bf16[8,128,128]{2,1,0:T(8,128)(2,1)S(1)}, u32[]{:S(2)}, u32[]{:S(2)}) async-start(bf16[8,128,128]{2,1,0:T(8,128)(2,1)} %bitcast.20), calls=%async_computation.3 | async-start | bytes 524288 | tf_op jit(solution)/shard_map/all_to_all | solution.py:403
  101.0 7.0 %collective-permute-start.4 = (bf16[2,3,128,128]{3,2,1,0:T(8,128)(2,1)S(1)}, bf16[2,3,128,128]{3,2,1,0:T(8,128)(2,1)S(1)}, u32[]{:S(2)}, u32[]{:S(2)}) collective-permute-start(bf16[2,3,128,128]{3,2,1,0:T(8,128)(2,1)S(1)} %slice.4), channel_id=1, source_target_pairs={{0,4},{4,8},{8,12},{12,16},{16,20},{20,24},{24,28},{1,5},{5,9},{9,... | collective-permute-start | bytes 589832 | tf_op jit(solution)/shard_map/ppermute | solution.py:406
  118.2 8.2 %collective-permute-start.5 = (bf16[2,3,128,128]{3,2,1,0:T(8,128)(2,1)S(1)}, bf16[2,3,128,128]{3,2,1,0:T(8,128)(2,1)S(1)}, u32[]{:S(2)}, u32[]{:S(2)}) collective-permute-start(bf16[2,3,128,128]{3,2,1,0:T(8,128)(2,1)S(1)} %get-tuple-element.31), channel_id=1, source_target_pairs={{4,0},{8,4},{12,8},{16,12},{20,16},{24,20},{28,24},{5,1},{9,5},{13... | collective-permute-start | bytes 589832 | tf_op jit(solution)/shard_map/ppermute | solution.py:409
  127.1 14.2 %all-to-all-start.4 = ((bf16[8,128,128]{2,1,0:T(8,128)(2,1)}), bf16[8,128,128]{2,1,0:T(8,128)(2,1)S(1)}, u32[]{:S(2)}, u32[]{:S(2)}) async-start(bf16[8,128,128]{2,1,0:T(8,128)(2,1)} %bitcast.10), calls=%async_computation.4 | async-start | bytes 524288 | tf_op jit(solution)/shard_map/all_to_all | solution.py:412
  141.3 1.6 copy-start.2
  148.8 24.5 %collective-permute-start.8 = (bf16[128,2048]{1,0:T(8,128)(2,1)}, bf16[128,2048]{1,0:T(8,128)(2,1)S(1)}, u32[]{:S(2)}, u32[]{:S(2)}) collective-permute-start(bf16[128,2048]{1,0:T(8,128)(2,1)} %get-tuple-element.36), channel_id=1, source_target_pairs={{0,128},{64,192},{128,0},{192,64},{1,129},{65,193},{129,1},{193,65... | collective-permute-start | bytes 1572872 | tf_op jit(solution)/shard_map/ppermute | solution.py:417
  158.6 18.9 %collective-permute-start.6 = (bf16[128,2048]{1,0:T(8,128)(2,1)}, bf16[128,2048]{1,0:T(8,128)(2,1)S(1)}, u32[]{:S(2)}, u32[]{:S(2)}) collective-permute-start(bf16[128,2048]{1,0:T(8,128)(2,1)} %get-tuple-element.34), channel_id=1, source_target_pairs={{0,64},{64,128},{128,192},{192,0},{1,65},{65,129},{129,193},{193,1... | collective-permute-start | bytes 1572872 | tf_op jit(solution)/shard_map/ppermute | solution.py:415
  160.8 16.8 %collective-permute-start.7 = (bf16[128,2048]{1,0:T(8,128)(2,1)}, bf16[128,2048]{1,0:T(8,128)(2,1)S(1)}, u32[]{:S(2)}, u32[]{:S(2)}) collective-permute-start(bf16[128,2048]{1,0:T(8,128)(2,1)} %get-tuple-element.35), channel_id=1, source_target_pairs={{0,192},{64,0},{128,64},{192,128},{1,193},{65,1},{129,65},{193,129... | collective-permute-start | bytes 1572872 | tf_op jit(solution)/shard_map/ppermute | solution.py:415
  165.1 18.2 %all-to-all-start.6 = ((bf16[32,16,128]{2,1,0:T(8,128)(2,1)}), bf16[32,16,128]{2,1,0:T(8,128)(2,1)S(1)}, u32[]{:S(2)}, u32[]{:S(2)}) async-start(bf16[32,16,128]{2,1,0:T(8,128)(2,1)} %get-tuple-element.37), calls=%async_computation.6 | async-start | bytes 262144 | tf_op jit(solution)/shard_map/all_to_all | solution.py:418

commit v4 on v3

--- a/solution.py
+++ b/solution.py
@@ -235,7 +235,7 @@
                 total = mix[i * 16 + a * 4] * grads[:, :HD]
                 for b in range(1, NPHM):
                     total = total + mix[i * 16 + a * 4 + b] * grads[:, b * HD : (b + 1) * HD]
-                mixed[n * HD : (n + 1) * HD, 2 * a * tok : 2 * (a + 1) * tok] = total.T.astype(BF16)
+                mixed[a, :, n * HD : (n + 1) * HD] = total.astype(BF16)
         if 0 in which:
             line = mixing_line(refs[0], grads)
             line = line + jnp.concatenate([line[:, HD // 2 :], line[:, : HD // 2]], axis=1)
@@ -243,7 +243,11 @@
             for d in range(refs[-1].shape[0]):
                 refs[-1][d] = line
 
-    total = dot(mixed[...], stacked(xs), 1, 0)
+    total = None
+    for a in range(NPHM):
+        x = jnp.concatenate([xs[a][0], xs[NPHM + a][0]], axis=0)
+        one = dot(mixed[a], x, 0, 0)
+        total = one if total is None else total + one
     outs = refs[1:3] if 0 in which else refs[:2]
     for n, out in enumerate(outs):
         out[...] = total[n * HD : (n + 1) * HD].astype(BF16)
@@ -270,7 +274,7 @@
         out_specs=out_specs,
         out_shape=out_shape,
         scratch_shapes=[
-            pltpu.VMEM((2 * HD, NPHM * 2 * tok), BF16),
+            pltpu.VMEM((NPHM, 2 * tok, 2 * HD), BF16),
             pltpu.VMEM((2 * tok, cols), F32),
         ],
         compiler_params=params(32),

time: 230 us -> 230 us (level)
  no operation moved by 1% of the time
where the time goes in v4:
time: 230 us; the launch traced here: 228 us
  waiting for transfers between devices  71.8 us (31%)
  starting transfers between devices  56.2 us (24%)
  blocking collectives  55.9 us (24%)
  Pallas kernels  28.3 us (12%)
  local copies, waits for them, and re-layouts  10 us (4%)
  other arithmetic  4.65 us (2%)
    all_to_all x1, blocking collectives, shards(): blocks = lax.all_to_all(total(blocks, lines, n_dp), DP, 0, 0, tiled=True)  26.1 us
    ppermute x1, waiting for transfers between devices, shards(): q2 = lax.ppermute(b2, 'zl', around(2))  23 us
    all_to_all x1, blocking collectives, shards(): blocks = lax.all_to_all(turn([own] + sent, n_ctx), CTX, 0, 0, tiled=True)  17.6 us
    all_to_all x1, blocking collectives, shards(): lax.all_to_all(piece, 'zl', 0, 0, tiled=True).reshape(1, n_z * rows, HD)  12.2 us
    pallas_call x2, Pallas kernels, factor_grads(): pl.pallas_call(functools.partial(factor_kernel, which), grid=(steps,), in...  10.7 us
    pallas_call x1, Pallas kernels, attend(): pl.pallas_call(attend_kernel, grid=(KVH,), in_specs=[SMEM, SMEM] + [whole...  10.2 us
    all_to_all x1, waiting for transfers between devices, shards(): lax.all_to_all(both.reshape(2 * KVH, tok, HD), ('c', 'zl'), 0, 0, tiled=T...  9.06 us
    all_to_all x1, waiting for transfers between devices, shards(): lax.all_to_all(grads, ('c', 'zl'), 0, 0, tiled=True)  8.94 us
  transfers between devices with their start and end apart: 14, of which 9 were waited for; matrix products, arithmetic and copies ran while one was open for 4% of the time, Pallas kernels for 5%

profile of v4, /device:TPU:1, one launch (start us, length us, event | category | flops | bytes accessed | tf_op | source)
XLA Modules:
  0.0 227.7 jit_solution(7885762992502799279)
XLA Ops:
  0.6 1.0 constant_dynamic-slice_fusion.6
  1.6 12.2 %all_to_all.40 = bf16[4,64,128]{2,1,0:T(8,128)(2,1)S(1)} all-to-all(bf16[4,64,128]{2,1,0:T(8,128)(2,1)S(1)} %broadcast_in_dim.23), channel_id=1, replica_groups=mesh['zh'=2,'x'=4,'c'=2,'y'=8,'zl'=4] {'zl'}, dimensions={0} | all-to-all | bytes 131072 | tf_op jit(solution)/shard_map/all_to_all | solution.py:392
  13.8 0.9 broadcast_in_dim.25
  14.7 6.8 %all-to-all-start.1 = ((bf16[8,256,128]{2,1,0:T(8,128)(2,1)}), bf16[8,256,128]{2,1,0:T(8,128)(2,1)S(1)}, u32[]{:S(2)}, u32[]{:S(2)}) async-start(bf16[8,256,128]{2,1,0:T(8,128)(2,1)} %broadcast_in_dim.25), calls=%async_computation.1 | async-start | bytes 1048576 | tf_op jit(solution)/shard_map/all_to_all | solution.py:393
  21.5 0.0 copy-start
  21.5 2.7 %constant_dynamic-slice_fusion = (bf16[1,128,1024]{2,1,0:T(8,128)(2,1)S(1)}, bf16[1,128,1024]{2,1,0:T(8,128)(2,1)S(1)}, bf16[1,128,1024]{2,1,0:T(8,128)(2,1)}, b...) fusion(bf16[1,128,4096]{2,1,0:T(8,128)(2,1)} %param.10, ...), kind=kLoop, calls=%fused_computation.11 | loop fusion | bytes 4194320 | tf_op jit(solution)/shard_map/dynamic_slice | solution.py:390
  24.2 0.1 pad_maximum_fusion.1
  24.3 2.5 %collective-permute-start.1 = (bf16[2,128,1024]{2,1,0:T(8,128)(2,1)S(1)}, bf16[2,128,1024]{2,1,0:T(8,128)(2,1)S(1)}, u32[]{:S(2)}, u32[]{:S(2)}) collective-permute-start(bf16[2,128,1024]{2,1,0:T(8,128)(2,1)S(1)} %pad_maximum_fusion.1), channel_id=1, source_target_pairs={{0,1},{1,2},{2,3},{3,0},{4,5},{5,6},{6,7},{7,4},{8,9},{9,10},{10,1... | collective-permute-start | bytes 1572872 | tf_op jit(solution)/shard_map/ppermute | solution.py:396
  26.9 0.0 copy-done
  26.9 4.6 %collective-permute-start = (bf16[1,128,8192]{2,1,0:T(8,128)(2,1)S(1)}, bf16[1,128,8192]{2,1,0:T(8,128)(2,1)}, u32[]{:S(2)}, u32[]{:S(2)}) collective-permute-start(bf16[1,128,8192]{2,1,0:T(8,128)(2,1)S(1)} %copy-done), channel_id=1, source_target_pairs={{0,32},{32,0},{1,33},{33,1},{2,34},{34,2},{3,35},{35,3},{4,36},{36... | collective-permute-start | bytes 6291464 | tf_op jit(solution)/shard_map/ppermute | solution.py:376
  31.4 0.8 pad_maximum_fusion.2
  32.3 6.7 %collective-permute-done.1.q1 = bf16[2,128,1024]{2,1,0:T(8,128)(2,1)S(1)} collective-permute-done((bf16[2,128,1024]{2,1,0:T(8,128)(2,1)S(1)}, bf16[2,128,1024]{2,1,0:T(8,128)(2,1)S(1)}, u32[]{:S(2)}, u32[]{:S(2)}) %collective-permute-start.1) | collective-permute-done | bytes 524320 | tf_op jit(solution)/shard_map/ppermute | solution.py:396
  39.0 0.0 all-to-all-done.1
  39.0 1.6 broadcast_in_dim.27
  40.7 0.0 copy-start.5
  40.7 0.0 copy-start.6
  40.7 4.6 %all-to-all-start.2 = ((bf16[4,2048,128]{2,1,0:T(8,128)(2,1)}), bf16[4,2048,128]{2,1,0:T(8,128)(2,1)}, u32[]{:S(2)}, u32[]{:S(2)}) async-start(bf16[4,2048,128]{2,1,0:T(8,128)(2,1)} %broadcast_in_dim.27), calls=%async_computation.2 | async-start | bytes 4194304 | tf_op jit(solution)/shard_map/all_to_all | solution.py:399
  45.3 1.9 collective-permute-start.2
  47.2 1.8 pad_maximum_fusion.3
  49.0 23.0 %collective-permute-done.2.q2 = bf16[2,128,1024]{2,1,0:T(8,128)(2,1)S(1)} collective-permute-done((bf16[2,128,1024]{2,1,0:T(8,128)(2,1)}, bf16[2,128,1024]{2,1,0:T(8,128)(2,1)S(1)}, u32[]{:S(2)}, u32[]{:S(2)}) %collective-permute-start.2) | collective-permute-done | bytes 524320 | tf_op jit(solution)/shard_map/ppermute | solution.py:398
  72.0 0.0 all-to-all-done.2.refs_8_
  72.0 1.9 collective-permute-start.3
  73.9 0.0 copy-done.5
  74.0 0.0 copy-done.6
  74.0 0.1 reshape.55.mix
  74.1 0.0 collective-permute-done.refs_4_.refs_5_.refs_6_.refs_7_
  74.1 0.0 copy-start.4
  74.1 6.1 %shard_map.111 = (f32[4,256,512]{2,1,0:T(8,128)S(1)}, bf16[2,4,128,128]{3,2,1,0:T(8,128)(2,1)S(1)}) custom-call(f32[64]{0:T(128)S(1)} %reshape.55.mix, s32[1]{0:T(128)} %bitcast.core, bf16[1,128,8192]{2,1,0:T(8,128)(2,1)S(1)} %copy-done, bf16[1,128,8192]{2,1,0:T(8,128)(2,1)S(1)} %copy-done, bf16[1,128,8192]{2,1,0:T(8,128)(2,1)S(1)} %copy-done, ...), custom_call_target="tpu_custom_call" | custom-call | tf_op jit(solution)/shard_map/pallas_call | solution.py:84
  80.2 0.0 copy-start.1
  80.2 1.3 copy-done.1
  81.5 0.0 copy-start.3
  81.5 0.7 copy-done.3
  82.2 4.9 %collective-permute-done.3.q3 = bf16[2,128,1024]{2,1,0:T(8,128)(2,1)} collective-permute-done((bf16[2,128,1024]{2,1,0:T(8,128)(2,1)}, bf16[2,128,1024]{2,1,0:T(8,128)(2,1)}, u32[]{:S(2)}, u32[]{:S(2)}) %collective-permute-start.3) | collective-permute-done | bytes 524320 | tf_op jit(solution)/shard_map/ppermute | solution.py:403
  87.1 4.8 %all-to-all-start.3 = ((bf16[8,128,128]{2,1,0:T(8,128)(2,1)}), bf16[8,128,128]{2,1,0:T(8,128)(2,1)S(1)}, u32[]{:S(2)}, u32[]{:S(2)}) async-start(bf16[8,128,128]{2,1,0:T(8,128)(2,1)} %bitcast.20), calls=%async_computation.3 | async-start | bytes 524288 | tf_op jit(solution)/shard_map/all_to_all | solution.py:407
  91.9 9.1 %all-to-all-done.3 = bf16[8,128,128]{2,1,0:T(8,128)(2,1)S(1)} async-done(((bf16[8,128,128]{2,1,0:T(8,128)(2,1)}), bf16[8,128,128]{2,1,0:T(8,128)(2,1)S(1)}, u32[]{:S(2)}, u32[]{:S(2)}) %all-to-all-start.3) | async-done | bytes 262176 | tf_op jit(solution)/shard_map/all_to_all | solution.py:407
  101.0 3.1 %collective-permute-start.4 = (bf16[2,3,128,128]{3,2,1,0:T(8,128)(2,1)S(1)}, bf16[2,3,128,128]{3,2,1,0:T(8,128)(2,1)S(1)}, u32[]{:S(2)}, u32[]{:S(2)}) collective-permute-start(bf16[2,3,128,128]{3,2,1,0:T(8,128)(2,1)S(1)} %slice.4), channel_id=1, source_target_pairs={{0,4},{4,8},{8,12},{12,16},{16,20},{20,24},{24,28},{1,5},{5,9},{9,... | collective-permute-start | bytes 589832 | tf_op jit(solution)/shard_map/ppermute | solution.py:410
  104.1 0.1 pad_add_fusion.where
  104.2 1.1 pad_maximum_fusion.q0
  105.3 2.8 %collective-permute-done.4.before = bf16[2,3,128,128]{3,2,1,0:T(8,128)(2,1)S(1)} collective-permute-done((bf16[2,3,128,128]{3,2,1,0:T(8,128)(2,1)S(1)}, bf16[2,3,128,128]{3,2,1,0:T(8,128)(2,1)S(1)}, u32[]{:S(2)}, u32[]{:S(2)}) %collective-permute-start.4) | collective-permute-done | bytes 196640 | tf_op jit(solution)/shard_map/ppermute | solution.py:410
  108.0 0.0 copy-done.4
  108.0 10.2 %shard_map.112 = (bf16[2,3,128,128]{3,2,1,0:T(8,128)(2,1)S(1)}, f32[2,4,128,128]{3,2,1,0:T(8,128)S(1)}) custom-call(s32[2]{0:T(128)S(1)} %pad_add_fusion.where, s32[32]{0:T(128)S(1)} %bitcast.21, bf16[2,128,1024]{2,1,0:T(8,128)(2,1)S(1)} %pad_maximum_fusion.q0, bf16[2,128,1024]{2,1,0:T(8,128)(2,1)S(1)} %collective-permute-done.1.q1, ...), custom_call_target="tpu_custom_call" | custom-call | tf_op jit(solution)/shard_map/pallas_call | solution.py:183
  118.2 1.3 collective-permute-start.5
  119.5 6.9 %collective-permute-done.5 = bf16[2,3,128,128]{3,2,1,0:T(8,128)(2,1)S(1)} collective-permute-done((bf16[2,3,128,128]{3,2,1,0:T(8,128)(2,1)S(1)}, bf16[2,3,128,128]{3,2,1,0:T(8,128)(2,1)S(1)}, u32[]{:S(2)}, u32[]{:S(2)}) %collective-permute-start.5) | collective-permute-done | bytes 196640 | tf_op jit(solution)/shard_map/ppermute | solution.py:413
  126.4 0.8 add_convert_fusion
  127.1 5.1 %all-to-all-start.4 = ((bf16[8,128,128]{2,1,0:T(8,128)(2,1)}), bf16[8,128,128]{2,1,0:T(8,128)(2,1)S(1)}, u32[]{:S(2)}, u32[]{:S(2)}) async-start(bf16[8,128,128]{2,1,0:T(8,128)(2,1)} %bitcast.10), calls=%async_computation.4 | async-start | bytes 524288 | tf_op jit(solution)/shard_map/all_to_all | solution.py:416
  132.3 0.1 reshape.52.mix
  132.4 8.9 %all-to-all-done.4 = bf16[8,128,128]{2,1,0:T(8,128)(2,1)S(1)} async-done(((bf16[8,128,128]{2,1,0:T(8,128)(2,1)}), bf16[8,128,128]{2,1,0:T(8,128)(2,1)S(1)}, u32[]{:S(2)}, u32[]{:S(2)}) %all-to-all-start.4) | async-done | bytes 262176 | tf_op jit(solution)/shard_map/all_to_all | solution.py:416
  141.3 0.0 copy-start.2
  141.3 1.6 copy-done.2
  142.9 5.7 %shard_map.113 = (bf16[128,2048]{1,0:T(8,128)(2,1)S(1)}, bf16[128,2048]{1,0:T(8,128)(2,1)}, bf16[32,16,128]{2,1,0:T(8,128)(2,1)}) custom-call(f32[64]{0:T(128)S(1)} %reshape.52.mix, s32[1]{0:T(128)} %bitcast.core, bf16[1,128,8192]{2,1,0:T(8,128)(2,1)S(1)} %copy-done, bf16[1,128,8192]{2,1,0:T(8,128)(2,1)S(1)} %copy-done, bf16[1,128,8192]{2,1,0:T(8,128)(2,1)S(1)} %copy-done, ...), custom_call_target="tpu_custom_call" | custom-call | tf_op jit(solution)/shard_map/pallas_call | solution.py:270
  148.6 4.7 %collective-permute-start.8 = (bf16[128,2048]{1,0:T(8,128)(2,1)}, bf16[128,2048]{1,0:T(8,128)(2,1)S(1)}, u32[]{:S(2)}, u32[]{:S(2)}) collective-permute-start(bf16[128,2048]{1,0:T(8,128)(2,1)} %get-tuple-element.36), channel_id=1, source_target_pairs={{0,128},{64,192},{128,0},{192,64},{1,129},{65,193},{129,1},{193,65... | collective-permute-start | bytes 1572872 | tf_op jit(solution)/shard_map/ppermute | solution.py:421
  153.3 5.0 %shard_map.114 = (bf16[128,2048]{1,0:T(8,128)(2,1)}, bf16[128,2048]{1,0:T(8,128)(2,1)}) custom-call(f32[64]{0:T(128)S(1)} %reshape.52.mix, s32[1]{0:T(128)} %bitcast.core, bf16[1,128,8192]{2,1,0:T(8,128)(2,1)S(1)} %copy-done, bf16[1,128,8192]{2,1,0:T(8,128)(2,1)S(1)} %copy-done, bf16[1,128,8192]{2,1,0:T(8,128)(2,1)S(1)} %copy-done, ...), custom_call_target="tpu_custom_call" | custom-call | tf_op jit(solution)/shard_map/pallas_call | solution.py:270
  158.3 2.2 collective-permute-start.6
  160.5 4.3 %collective-permute-start.7 = (bf16[128,2048]{1,0:T(8,128)(2,1)}, bf16[128,2048]{1,0:T(8,128)(2,1)S(1)}, u32[]{:S(2)}, u32[]{:S(2)}) collective-permute-start(bf16[128,2048]{1,0:T(8,128)(2,1)} %get-tuple-element.35), channel_id=1, source_target_pairs={{0,192},{64,0},{128,64},{192,128},{1,193},{65,1},{129,65},{193,129... | collective-permute-start | bytes 1572872 | tf_op jit(solution)/shard_map/ppermute | solution.py:419
  164.8 8.3 %all-to-all-start.6 = ((bf16[32,16,128]{2,1,0:T(8,128)(2,1)}), bf16[32,16,128]{2,1,0:T(8,128)(2,1)S(1)}, u32[]{:S(2)}, u32[]{:S(2)}) async-start(bf16[32,16,128]{2,1,0:T(8,128)(2,1)} %get-tuple-element.37), calls=%async_computation.6 | async-start | bytes 262144 | tf_op jit(solution)/shard_map/all_to_all | solution.py:422
  173.1 0.0 collective-permute-done.8.t3
  173.1 4.1 %collective-permute-done.6.t1 = bf16[128,2048]{1,0:T(8,128)(2,1)S(1)} collective-permute-done((bf16[128,2048]{1,0:T(8,128)(2,1)}, bf16[128,2048]{1,0:T(8,128)(2,1)S(1)}, u32[]{:S(2)}, u32[]{:S(2)}) %collective-permute-start.6) | collective-permute-done | bytes 524320 | tf_op jit(solution)/shard_map/ppermute | solution.py:419
  177.3 0.0 collective-permute-done.7.t2
  177.3 0.4 shard_map.115
  177.6 5.4 %all-to-all-done.6.lines = bf16[32,16,128]{2,1,0:T(8,128)(2,1)S(1)} async-done(((bf16[32,16,128]{2,1,0:T(8,128)(2,1)}), bf16[32,16,128]{2,1,0:T(8,128)(2,1)S(1)}, u32[]{:S(2)}, u32[]{:S(2)}) %all-to-all-start.6) | async-done | bytes 131104 | tf_op jit(solution)/shard_map/all_to_all | solution.py:422
  183.0 17.6 %all_to_all.41.blocks = bf16[32,64,128]{2,1,0:T(8,128)(2,1)S(1)} all-to-all(bf16[32,64,128]{2,1,0:T(8,128)(2,1)S(1)} %shard_map.115), channel_id=1, replica_groups=mesh['zh'=2,'x'=4,'c'=2,'y'=8,'zl'=4] {'y','zl'}, dimensions={0} | all-to-all | bytes 1048576 | tf_op jit(solution)/shard_map/all_to_all | solution.py:423
  200.7 0.1 shard_map.116
  200.8 26.1 %all_to_all.42.blocks = bf16[16,80,128]{2,1,0:T(8,128)(2,1)S(1)} all-to-all(bf16[16,80,128]{2,1,0:T(8,128)(2,1)S(1)} %shard_map.116), channel_id=1, replica_groups=mesh['zh'=2,'x'=4,'c'=2,'y'=8,'zl'=4] {'zh','x','c'}, dimensions={0} | all-to-all | bytes 655360 | tf_op jit(solution)/shard_map/all_to_all | solution.py:424
  226.9 0.8 shard_map.117
  (5 shorter events, 0.1 us)
Async XLA Ops:
  14.7 24.3 %all-to-all-start.1 = ((bf16[8,256,128]{2,1,0:T(8,128)(2,1)}), bf16[8,256,128]{2,1,0:T(8,128)(2,1)S(1)}, u32[]{:S(2)}, u32[]{:S(2)}) async-start(bf16[8,256,128]{2,1,0:T(8,128)(2,1)} %broadcast_in_dim.25), calls=%async_computation.1 | async-start | bytes 1048576 | tf_op jit(solution)/shard_map/all_to_all | solution.py:393
  21.5 5.3 %copy-start = (bf16[1,128,8192]{2,1,0:T(8,128)(2,1)S(1)}, bf16[1,128,8192]{2,1,0:T(8,128)(2,1)}, u32[]{:S(2)}) copy-start(bf16[1,128,8192]{2,1,0:T(8,128)(2,1)} %refs_3_.5) | copy-start | bytes 6291460
  24.3 14.7 %collective-permute-start.1 = (bf16[2,128,1024]{2,1,0:T(8,128)(2,1)S(1)}, bf16[2,128,1024]{2,1,0:T(8,128)(2,1)S(1)}, u32[]{:S(2)}, u32[]{:S(2)}) collective-permute-start(bf16[2,128,1024]{2,1,0:T(8,128)(2,1)S(1)} %pad_maximum_fusion.1), channel_id=1, source_target_pairs={{0,1},{1,2},{2,3},{3,0},{4,5},{5,6},{6,7},{7,4},{8,9},{9,10},{10,1... | collective-permute-start | bytes 1572872 | tf_op jit(solution)/shard_map/ppermute | solution.py:396
  26.9 47.2 %collective-permute-start = (bf16[1,128,8192]{2,1,0:T(8,128)(2,1)S(1)}, bf16[1,128,8192]{2,1,0:T(8,128)(2,1)}, u32[]{:S(2)}, u32[]{:S(2)}) collective-permute-start(bf16[1,128,8192]{2,1,0:T(8,128)(2,1)S(1)} %copy-done), channel_id=1, source_target_pairs={{0,32},{32,0},{1,33},{33,1},{2,34},{34,2},{3,35},{35,3},{4,36},{36... | collective-permute-start | bytes 6291464 | tf_op jit(solution)/shard_map/ppermute | solution.py:376
  40.7 33.3 %copy-start.5 = (f32[4,4,4]{2,1,0:T(4,128)S(1)}, f32[4,4,4]{2,1,0:T(4,128)}, u32[]{:S(2)}) copy-start(f32[4,4,4]{2,1,0:T(4,128)} %param.14) | copy-start | bytes 772
  40.7 33.3 %copy-start.6 = (f32[4,4,4]{2,1,0:T(4,128)S(1)}, f32[4,4,4]{2,1,0:T(4,128)}, u32[]{:S(2)}) copy-start(f32[4,4,4]{2,1,0:T(4,128)} %param.15) | copy-start | bytes 772
  40.7 31.3 %all-to-all-start.2 = ((bf16[4,2048,128]{2,1,0:T(8,128)(2,1)}), bf16[4,2048,128]{2,1,0:T(8,128)(2,1)}, u32[]{:S(2)}, u32[]{:S(2)}) async-start(bf16[4,2048,128]{2,1,0:T(8,128)(2,1)} %broadcast_in_dim.27), calls=%async_computation.2 | async-start | bytes 4194304 | tf_op jit(solution)/shard_map/all_to_all | solution.py:399
  45.3 26.7 %collective-permute-start.2 = (bf16[2,128,1024]{2,1,0:T(8,128)(2,1)}, bf16[2,128,1024]{2,1,0:T(8,128)(2,1)S(1)}, u32[]{:S(2)}, u32[]{:S(2)}) collective-permute-start(bf16[2,128,1024]{2,1,0:T(8,128)(2,1)} %pad_maximum_fusion.2), channel_id=1, source_target_pairs={{0,2},{1,3},{2,0},{3,1},{4,6},{5,7},{6,4},{7,5},{8,10},{9,11},{10,... | collective-permute-start | bytes 1572872 | tf_op jit(solution)/shard_map/ppermute | solution.py:398
  72.0 15.1 %collective-permute-start.3 = (bf16[2,128,1024]{2,1,0:T(8,128)(2,1)}, bf16[2,128,1024]{2,1,0:T(8,128)(2,1)}, u32[]{:S(2)}, u32[]{:S(2)}) collective-permute-start(bf16[2,128,1024]{2,1,0:T(8,128)(2,1)} %pad_maximum_fusion.3), channel_id=1, source_target_pairs={{0,3},{1,0},{2,1},{3,2},{4,7},{5,4},{6,5},{7,6},{8,11},{9,8},{10,9... | collective-permute-start | bytes 1572872 | tf_op jit(solution)/shard_map/ppermute | solution.py:403
  74.1 33.9 %copy-start.4 = (s32[1,32]{1,0:T(1,128)S(1)}, s32[1,32]{1,0:T(1,128)}, u32[]{:S(2)}) copy-start(s32[1,32]{1,0:T(1,128)} %param.11) | copy-start | bytes 388
  80.2 1.3 copy-start.1
  81.5 0.7 copy-start.3
  87.1 13.9 %all-to-all-start.3 = ((bf16[8,128,128]{2,1,0:T(8,128)(2,1)}), bf16[8,128,128]{2,1,0:T(8,128)(2,1)S(1)}, u32[]{:S(2)}, u32[]{:S(2)}) async-start(bf16[8,128,128]{2,1,0:T(8,128)(2,1)} %bitcast.20), calls=%async_computation.3 | async-start | bytes 524288 | tf_op jit(solution)/shard_map/all_to_all | solution.py:407
  101.0 7.0 %collective-permute-start.4 = (bf16[2,3,128,128]{3,2,1,0:T(8,128)(2,1)S(1)}, bf16[2,3,128,128]{3,2,1,0:T(8,128)(2,1)S(1)}, u32[]{:S(2)}, u32[]{:S(2)}) collective-permute-start(bf16[2,3,128,128]{3,2,1,0:T(8,128)(2,1)S(1)} %slice.4), channel_id=1, source_target_pairs={{0,4},{4,8},{8,12},{12,16},{16,20},{20,24},{24,28},{1,5},{5,9},{9,... | collective-permute-start | bytes 589832 | tf_op jit(solution)/shard_map/ppermute | solution.py:410
  118.2 8.2 %collective-permute-start.5 = (bf16[2,3,128,128]{3,2,1,0:T(8,128)(2,1)S(1)}, bf16[2,3,128,128]{3,2,1,0:T(8,128)(2,1)S(1)}, u32[]{:S(2)}, u32[]{:S(2)}) collective-permute-start(bf16[2,3,128,128]{3,2,1,0:T(8,128)(2,1)S(1)} %get-tuple-element.31), channel_id=1, source_target_pairs={{4,0},{8,4},{12,8},{16,12},{20,16},{24,20},{28,24},{5,1},{9,5},{13... | collective-permute-start | bytes 589832 | tf_op jit(solution)/shard_map/ppermute | solution.py:413
  127.1 14.2 %all-to-all-start.4 = ((bf16[8,128,128]{2,1,0:T(8,128)(2,1)}), bf16[8,128,128]{2,1,0:T(8,128)(2,1)S(1)}, u32[]{:S(2)}, u32[]{:S(2)}) async-start(bf16[8,128,128]{2,1,0:T(8,128)(2,1)} %bitcast.10), calls=%async_computation.4 | async-start | bytes 524288 | tf_op jit(solution)/shard_map/all_to_all | solution.py:416
  141.3 1.6 copy-start.2
  148.6 24.5 %collective-permute-start.8 = (bf16[128,2048]{1,0:T(8,128)(2,1)}, bf16[128,2048]{1,0:T(8,128)(2,1)S(1)}, u32[]{:S(2)}, u32[]{:S(2)}) collective-permute-start(bf16[128,2048]{1,0:T(8,128)(2,1)} %get-tuple-element.36), channel_id=1, source_target_pairs={{0,128},{64,192},{128,0},{192,64},{1,129},{65,193},{129,1},{193,65... | collective-permute-start | bytes 1572872 | tf_op jit(solution)/shard_map/ppermute | solution.py:421
  158.3 19.0 %collective-permute-start.6 = (bf16[128,2048]{1,0:T(8,128)(2,1)}, bf16[128,2048]{1,0:T(8,128)(2,1)S(1)}, u32[]{:S(2)}, u32[]{:S(2)}) collective-permute-start(bf16[128,2048]{1,0:T(8,128)(2,1)} %get-tuple-element.34), channel_id=1, source_target_pairs={{0,64},{64,128},{128,192},{192,0},{1,65},{65,129},{129,193},{193,1... | collective-permute-start | bytes 1572872 | tf_op jit(solution)/shard_map/ppermute | solution.py:419
  160.5 16.8 %collective-permute-start.7 = (bf16[128,2048]{1,0:T(8,128)(2,1)}, bf16[128,2048]{1,0:T(8,128)(2,1)S(1)}, u32[]{:S(2)}, u32[]{:S(2)}) collective-permute-start(bf16[128,2048]{1,0:T(8,128)(2,1)} %get-tuple-element.35), channel_id=1, source_target_pairs={{0,192},{64,0},{128,64},{192,128},{1,193},{65,1},{129,65},{193,129... | collective-permute-start | bytes 1572872 | tf_op jit(solution)/shard_map/ppermute | solution.py:419
  164.8 18.2 %all-to-all-start.6 = ((bf16[32,16,128]{2,1,0:T(8,128)(2,1)}), bf16[32,16,128]{2,1,0:T(8,128)(2,1)S(1)}, u32[]{:S(2)}, u32[]{:S(2)}) async-start(bf16[32,16,128]{2,1,0:T(8,128)(2,1)} %get-tuple-element.37), calls=%async_computation.6 | async-start | bytes 262144 | tf_op jit(solution)/shard_map/all_to_all | solution.py:422
